TPU v7x, 32 devices: a whole 2x2x4 slice. The times are simulated.
32 devices in a mesh: seq: 8 (over y, x, core), tp: 4 (over z).
Axes of the slice: x: 2, y: 2, z: 4, core: 2. Of those that a mesh axis runs over, the one named last changes fastest.
Arguments:
- inputs: bfloat16 [16384, 1024], P(('seq', 'tp')), may hold values from -6 to 6
- segment_ids: int32 [8, 2048], P('seq'), may hold values from 0 to 5, never falling along the last dimension, each value on 1 to 512 neighbouring positions
- row_lengths: int32 [8], P('seq'), may hold values from 1536 to 2048
- norm1_gain: float32 [1024], replicated, may hold values from 0.5 to 1.5
- norm1_shift: float32 [1024], replicated, may hold values from -4 to 4
- w_query: bfloat16 [1024, 1024], P(None, 'tp'), may hold values from -0.1875 to 0.1875
- w_key: bfloat16 [1024, 1024], P(None, 'tp'), may hold values from -0.1875 to 0.1875
- w_value: bfloat16 [1024, 1024], P(None, 'tp'), may hold values from -0.1875 to 0.1875
- b_query: float32 [1024], P('tp'), may hold values from -6 to 6
- b_value: float32 [1024], P('tp'), may hold values from -6 to 6
- w_out: bfloat16 [1024, 1024], P('tp'), may hold values from -2 to 2
- b_out: float32 [1024], replicated, may hold values from -6 to 6
- norm2_gain: float32 [1024], replicated, may hold values from 0.5 to 1.5
- norm2_shift: float32 [1024], replicated, may hold values from -4 to 4
- w_up: bfloat16 [1024, 1024], P(None, 'tp'), may hold values from -0.1875 to 0.1875
- b_up: float32 [1024], P('tp'), may hold values from -6 to 6
- w_down: bfloat16 [1024, 1024], P('tp'), may hold values from -0.1875 to 0.1875
- b_down: float32 [1024], replicated, may hold values from -6 to 6
- out_grad: bfloat16 [16384, 1024], P(('seq', 'tp')), may hold values from -6 to 6
Outputs:
- output: bfloat16 [16384, 1024], P(('seq', 'tp'))
- grad_inputs: bfloat16 [16384, 1024], P(('seq', 'tp'))
- grad_norm1_gain: float32 [1024], replicated
- grad_norm1_shift: float32 [1024], replicated
- grad_w_query: float32 [1024, 1024], P(None, 'tp')
- grad_w_key: float32 [1024, 1024], P(None, 'tp')
- grad_w_value: float32 [1024, 1024], P(None, 'tp')
- grad_b_query: float32 [1024], P('tp')
- grad_b_value: float32 [1024], P('tp')
- grad_w_out: float32 [1024, 1024], P('tp')
- grad_b_out: float32 [1024], replicated
- grad_norm2_gain: float32 [1024], replicated
- grad_norm2_shift: float32 [1024], replicated
- grad_w_up: float32 [1024, 1024], P(None, 'tp')
- grad_b_up: float32 [1024], P('tp')
- grad_w_down: float32 [1024, 1024], P('tp')
- grad_b_down: float32 [1024], replicated
Inputs may be any that keep to these rules, and one draw needn't show every extreme that they name: `segment_ids`: along a row segment numbers never fall, and one number covers at most 512 positions; positions at or past a row's length are padding.
All inputs are finite; a program needn't handle non-finite values.
Results may differ from a plain program's by a relative error of at most 0.018.
Values may be sent and summed in bfloat16 or wider, within the bound.
No kernel may reach another device: no remote copies, remote signals or barrier semaphores. Data moves between devices by JAX's collectives and lax.ppermute only.
A program may use at most 128 MiB of HBM per device.

v0:
```python
import functools
import math

import jax
import jax.numpy as jnp
from jax import lax
from jax.experimental import pallas as pl
from jax.experimental.pallas import tpu as pltpu
from jax.sharding import PartitionSpec as P

HEAD_DIM = 128
ROW_LEN = 2048
NORM_EPS = 1e-05
MASKED = -1000000000.0
LOG2E = 1.4426950408889634
TILE = 256
BLOCK = 256
FAR = 256
ROWS = 128
GROUPS = 1
F32 = jnp.float32
BF16 = jnp.bfloat16
VMEM_LIMIT = 58 * 1024 * 1024


def dot_nn(a, b):
    return lax.dot_general(a, b, (((1,), (0,)), ((), ())), preferred_element_type=F32)


def dot_nt(a, b):
    return lax.dot_general(a, b, (((1,), (1,)), ((), ())), preferred_element_type=F32)


def dot_tn(a, b):
    return lax.dot_general(a, b, (((0,), (0,)), ((), ())), preferred_element_type=F32)


def normalise(x):
    centre = x - jnp.mean(x, axis=-1, keepdims=True)
    rstd = lax.rsqrt(jnp.mean(centre * centre, axis=-1, keepdims=True) + NORM_EPS)
    return centre * rstd, rstd


def norm_back(grad, hat, rstd, gain):
    t = gain * grad
    mean_t = jnp.mean(t, axis=-1, keepdims=True)
    mean_th = jnp.mean(t * hat, axis=-1, keepdims=True)
    return (t - mean_t - hat * mean_th) * rstd


def call(kernel, outs, ins, scratch, name, smem=0, anys=0, out_anys=0, gflop=50):
    spaces = [pltpu.SMEM] * smem + [pltpu.VMEM] * (len(ins) - smem - anys) + [pl.ANY] * anys
    out_spaces = [pltpu.VMEM] * (len(outs) - out_anys) + [pl.ANY] * out_anys
    return pl.pallas_call(
        kernel,
        out_shape=tuple(jax.ShapeDtypeStruct(*o) for o in outs),
        in_specs=[pl.BlockSpec(memory_space=m) for m in spaces],
        out_specs=tuple(pl.BlockSpec(memory_space=m) for m in out_spaces),
        scratch_shapes=scratch,
        compiler_params=pltpu.CompilerParams(vmem_limit_bytes=VMEM_LIMIT),
        cost_estimate=pl.CostEstimate(
            flops=gflop * 10**9, bytes_accessed=1000000, transcendentals=0
        ),
        name=name,
    )(*ins)


def load_weights(meta, shards, off, pieces, dst, sem):
    s, t = meta[0], meta[1]
    count, size, per = pieces[0].shape[1:]
    n_tp = dst.shape[2] // per
    if len(pieces) == 1:
        for i in range(pieces[0].shape[0]):
            at, to = i // n_tp * size, i % n_tp * per
            target = dst.at[:, at : at + size, to : to + per]
            pltpu.make_async_copy(pieces[0].at[i], target, sem).start()
        return pltpu.make_async_copy(dst, dst, sem).wait
    mine = pl.ds(pl.multiple_of(t * per, per), per)
    for m in range(count):
        source = shards[m].at[:, off : off + per]
        pltpu.make_async_copy(source, dst.at[m, :, mine], sem).start()
    for j, piece in enumerate(pieces):
        at = pl.ds(pl.multiple_of((s ^ j) * size, size), size)
        for r in range(n_tp - 1):
            u = pl.multiple_of(lax.rem(t + r + 1, n_tp) * per, per)
            pltpu.make_async_copy(piece.at[r], dst.at[:, at, pl.ds(u, per)], sem).start()
    return pltpu.make_async_copy(dst, dst, sem).wait


def store_grads(meta, grads, keep, send, sems, first, last):
    s = meta[0]
    half, n_tp, _, size, per = keep.shape
    for parity, dst in enumerate((keep, send)):
        for jj in range(half):
            p = pl.ds(pl.multiple_of((s ^ (2 * jj + parity)) * size, size), size)
            for t in range(n_tp):
                pltpu.make_async_copy(
                    grads.at[first:last, p, t * per : (t + 1) * per],
                    dst.at[jj, t, first:last],
                    sems.at[parity],
                ).start()


def grads_stored(keep, send, sems):
    for parity, dst in enumerate((keep, send)):
        pltpu.make_async_copy(dst, dst, sems.at[parity]).wait()


def attend(rng, segq, segk, q, k, v, mixed, lse, s_scr, m_scr, l_scr, acc):
    heads = q.shape[1] // HEAD_DIM
    coef = HEAD_DIM**-0.5 * LOG2E
    of = [slice(h * HEAD_DIM, (h + 1) * HEAD_DIM) for h in range(heads)]

    def fold(x, op):
        x = x.reshape(BLOCK // 8, 8, BLOCK)
        res = x[0]
        for i in range(1, BLOCK // 8):
            res = op(res, x[i])
        return res

    @pl.loop(0, q.shape[0] // BLOCK)
    def _(qb):
        rows = pl.ds(pl.multiple_of(qb * BLOCK, BLOCK), BLOCK)
        lo = rng[0, qb]
        hi = rng[1, qb]
        sq = segq[:, rows]
        m_scr[...] = jnp.full(m_scr.shape, -3e38, F32)
        l_scr[...] = jnp.zeros(l_scr.shape, F32)
        acc[...] = jnp.zeros(acc.shape, F32)

        @pl.loop(lo, hi)
        def _(kc):
            ks = pl.ds(pl.multiple_of(kc * BLOCK, BLOCK), BLOCK)
            bias = jnp.where(segk[ks, :] == sq, 0.0, MASKED)
            for h in range(0, heads, 2):
                pair = (h, h + 1)
                scores = [dot_nt(k[ks, of[i]], q[rows, of[i]]) * coef + bias for i in pair]
                for i, s in zip(pair, scores):
                    s_scr[kc, i] = s
                    m_scr[i] = jnp.maximum(m_scr[i], fold(s, jnp.maximum))

        for h in range(heads):
            m_scr[h] = jnp.broadcast_to(jnp.max(m_scr[h], axis=0, keepdims=True), (8, BLOCK))

        @pl.loop(lo, hi)
        def _(kc):
            ks = pl.ds(pl.multiple_of(kc * BLOCK, BLOCK), BLOCK)
            for h in range(0, heads, 2):
                pair = (h, h + 1)
                probs = [jnp.exp2(s_scr[kc, i] - m_scr[i, :1]) for i in pair]
                outs = [dot_tn(v[ks, of[i]], p.astype(BF16)) for i, p in zip(pair, probs)]
                for i, p, o in zip(pair, probs, outs):
                    l_scr[i] += fold(p, jnp.add)
                    acc[i] += o

        for h in range(heads):
            total = jnp.sum(l_scr[h], axis=0, keepdims=True)
            mixed[rows, of[h]] = jnp.transpose(acc[h] / total).astype(BF16)
            lse[h : h + 1, rows] = m_scr[h, :1] + jnp.log2(total)


def attend_back(rng, segq, segk, lse, delta, q, do, k, v, dq, dk_acc, dv_acc, dq_acc):
    heads = q.shape[1] // HEAD_DIM
    scale = HEAD_DIM**-0.5
    coef = scale * LOG2E
    of = [slice(h * HEAD_DIM, (h + 1) * HEAD_DIM) for h in range(heads)]

    @pl.loop(0, q.shape[0] // BLOCK)
    def _(qb):
        rows = pl.ds(pl.multiple_of(qb * BLOCK, BLOCK), BLOCK)
        lo = rng[0, qb]
        hi = rng[1, qb]
        sq = segq[:, rows]
        dq_acc[...] = jnp.zeros(dq_acc.shape, F32)

        @pl.loop(lo, hi)
        def _(kc):
            ks = pl.ds(pl.multiple_of(kc * BLOCK, BLOCK), BLOCK)
            bias = jnp.where(segk[ks, :] == sq, 0.0, MASKED)

            def probs(h):
                s = dot_nt(k[ks, of[h]], q[rows, of[h]]) * coef
                p = jnp.exp2(s + (bias - lse[h : h + 1, rows]))
                return p, dot_nt(v[ks, of[h]], do[rows, of[h]])

            def products(h, p, dp):
                ds = (p * (dp - delta[h : h + 1, rows])).astype(BF16)
                return (
                    dot_nn(p.astype(BF16), do[rows, of[h]]),
                    dot_nn(ds, q[rows, of[h]]),
                    dot_tn(k[ks, of[h]], ds),
                )

            for h in range(0, heads, 2):
                pair = (h, h + 1)
                both = [probs(i) for i in pair]
                terms = [products(i, *b) for i, b in zip(pair, both)]
                for i, (a, b, c) in zip(pair, terms):
                    dv_acc[ks, of[i]] += a
                    dk_acc[ks, of[i]] += b
                    dq_acc[i] += c

        for h in range(heads):
            dq[rows, of[h]] = (jnp.transpose(dq_acc[h]) * scale).astype(BF16)


def used_chunks(rng):
    tokens = BLOCK * rng.shape[1]
    before = rng[0, 0] * BLOCK < tokens - FAR
    after = rng[1, rng.shape[1] - 1] * BLOCK > 2 * tokens + FAR
    return before, after


def forward_kernel(first, n_pieces, off, meta, rng, segq, segk, *refs):
    if first:
        gain, shift, bq, bv, left, own, right, *refs = refs
    else:
        bq, bv, low_in, *refs = refs
    shards, pieces, refs = refs[:3], refs[3 : 3 + n_pieces], refs[3 + n_pieces :]
    mixed, lse, q_out, k_out, v_out, *refs = refs
    if first:
        low_out, *refs = refs
    q, k, v, low, w, s_scr, m_scr, l_scr, acc, sem, out_sems, *refs = refs
    tokens = q.shape[0]
    before, after = used_chunks(rng)
    lo = jnp.where(before, 0, (tokens - FAR) // BLOCK)
    hi = jnp.where(after, 3 * tokens, 2 * tokens + FAR) // BLOCK

    def copy(i, src, dst):
        return pltpu.make_async_copy(src, dst, out_sems.at[i])

    def chunk(c):
        return pl.ds(pl.multiple_of(c * BLOCK, BLOCK), BLOCK)

    if first:
        (window,) = refs
        ins = [
            copy(i, x, window.at[i * tokens : (i + 1) * tokens])
            for i, x in enumerate((left, own, right))
        ]
    else:
        ins = [copy(3, low_in, low)]
    for x in ins:
        x.start()
    wait = load_weights(meta, shards, off, pieces, w, sem)
    for x in ins:
        x.wait()
    outs = [(q, q_out), (k, k_out), (v, v_out)]
    if first:

        @pl.loop(lo, hi)
        def _(c):
            hat, _ = normalise(window[chunk(c), :].astype(F32))
            low[chunk(c), :] = (hat * gain[...] + shift[...]).astype(BF16)

        outs.append((low, low_out))
        copy(3, *outs[3]).start()
    wait()
    q[...] = (dot_nn(low[tokens : 2 * tokens, :], w[0]) + bq[...]).astype(BF16)
    copy(0, *outs[0]).start()

    @pl.loop(lo, hi)
    def _(c):
        k[chunk(c), :] = dot_nn(low[chunk(c), :], w[1]).astype(BF16)
        v[chunk(c), :] = (dot_nn(low[chunk(c), :], w[2]) + bv[...]).astype(BF16)

    copy(1, *outs[1]).start()
    copy(2, *outs[2]).start()
    attend(rng, segq, segk, q, k, v, mixed, lse, s_scr, m_scr, l_scr, acc)
    for i, x in enumerate(outs):
        copy(i, *x).wait()


def forward(group, meta, rng, segq, segk, source, bq, bv, shards, pieces):
    first = group == 0
    width = shards[0].shape[0]
    window = segk.shape[0]
    tokens = window // 3
    per = pieces[0].shape[3]
    cols = bq.shape[1]
    heads = cols // HEAD_DIM
    slim, wide = (tokens, cols), (window, cols)
    kept = ((window, width), BF16)
    ins = [meta, rng, segq, segk]
    ins += [*source[:2], bq, bv, *source[2:]] if first else [bq, bv, source]
    return call(
        functools.partial(forward_kernel, first, len(pieces), group * per),
        [(slim, BF16), ((heads, tokens), F32), (slim, BF16), (wide, BF16), (wide, BF16)]
        + [kept] * first,
        [*ins, *shards, *pieces],
        [
            pltpu.VMEM(slim, BF16),
            pltpu.VMEM(wide, BF16),
            pltpu.VMEM(wide, BF16),
            pltpu.VMEM(*kept),
            pltpu.VMEM((3, width, cols), BF16),
            pltpu.VMEM((window // BLOCK, heads, BLOCK, BLOCK), F32),
            pltpu.VMEM((heads, 8, BLOCK), F32),
            pltpu.VMEM((heads, 8, BLOCK), F32),
            pltpu.VMEM((heads, HEAD_DIM, BLOCK), F32),
            pltpu.SemaphoreType.DMA,
            pltpu.SemaphoreType.DMA((4,)),
        ]
        + [pltpu.VMEM(*kept)] * first,
        "forward_attention",
        smem=2,
        anys=3 + len(pieces) + (3 if first else 1),
        out_anys=3 + first,
    )


def feed_kernel(n_pieces, groups, meta, inputs, dout, bo, gain, shift, bup, bdn, *refs):
    parts, refs = refs[:groups], refs[groups:]
    pieces, refs = refs[:n_pieces], refs[n_pieces:]
    g_parts, refs = refs[:groups], refs[groups:]
    deltas, refs = refs[:groups], refs[groups:]
    sums, output_out, g_resid_out, keep, send, *refs = refs
    w, mixed, resid, hat, rstd, second, hidden, g_up, g_sec, low, output, grads, *sems = refs
    sem, grad_sems, out_sems = sems
    wait = load_weights(meta, None, 0, pieces, w, sem)
    wo_t, wup, wdn_t = w.at[0], w.at[1], w.at[2]
    tokens, width = inputs.shape
    per = SHARD // groups
    for g in range(groups):
        for t in range(width // SHARD):
            at = t * SHARD + g * per
            mixed[:, at : at + per] = parts[g][:, t * per : (t + 1) * per]
    sums[...] = jnp.zeros(sums.shape, F32)
    sums[4:5, :] = jnp.sum(dout[...].astype(F32), axis=0, keepdims=True)
    wait()
    resid[...] = inputs[...].astype(F32) + dot_nt(mixed[...], wo_t[...]) + bo[...]

    @pl.loop(0, tokens // BLOCK)
    def _(i):
        rows = pl.ds(pl.multiple_of(i * BLOCK, BLOCK), BLOCK)
        h, r = normalise(resid[rows, :])
        hat[rows, :] = h
        rstd[rows, :] = jnp.broadcast_to(r, (BLOCK, 128))
        second[rows, :] = (h * gain[...] + shift[...]).astype(BF16)

    for n in range(width // TILE):
        cols = slice(n * TILE, (n + 1) * TILE)
        up = dot_nn(second[...], wup[:, cols]) + bup[:, cols]
        d_hidden = dot_nn(dout[...], wdn_t[:, cols])
        phi = 0.5 + 0.5 * lax.erf(up * (0.5**0.5))
        hidden[:, cols] = (up * phi).astype(BF16)
        slope = phi + up * (jnp.exp(-0.5 * up * up) * (0.5 / math.pi) ** 0.5)
        grad = (d_hidden * slope).astype(BF16)
        g_up[:, cols] = grad
        sums[3:4, cols] = jnp.sum(grad.astype(F32), axis=0, keepdims=True)
    g_sec[...] = dot_nt(g_up[...], wup[...])
    output[...] = (resid[...] + dot_nt(hidden[...], wdn_t[...]) + bdn[...]).astype(BF16)
    out_copy = pltpu.make_async_copy(output, output_out, out_sems.at[0])
    out_copy.start()
    grads[2] = dot_tn(dout[...], hidden[...]).astype(BF16)
    grads[1] = dot_tn(second[...], g_up[...]).astype(BF16)
    store_grads(meta, grads, keep, send, grad_sems, 1, 3)

    @pl.loop(0, tokens // ROWS)
    def _(i):
        rows = pl.ds(pl.multiple_of(i * ROWS, ROWS), ROWS)
        h, g = hat[rows, :], g_sec[rows, :]
        res = dout[rows, :].astype(F32) + norm_back(g, h, rstd[rows, :1], gain[...])
        resid[rows, :] = res
        low[rows, :] = res.astype(BF16)
        for n, x in enumerate((res, g * h, g)):
            sums[n : n + 1, :] += jnp.sum(x, axis=0, keepdims=True)

    resid_copy = pltpu.make_async_copy(resid, g_resid_out, out_sems.at[1])
    resid_copy.start()
    grads[0] = dot_tn(low[...], mixed[...]).astype(BF16)
    store_grads(meta, grads, keep, send, grad_sems, 0, 1)
    ones = jnp.ones((8, HEAD_DIM), BF16)
    for n in range(width // TILE):
        cols = slice(n * TILE, (n + 1) * TILE)
        grad = dot_nn(low[...], wo_t[:, cols]).astype(BF16)
        prod = grad.astype(F32) * mixed[:, cols].astype(F32)
        high = prod.astype(BF16)
        rest_of = (prod - high.astype(F32)).astype(BF16)
        for i in range(TILE // HEAD_DIM):
            part = slice(i * HEAD_DIM, (i + 1) * HEAD_DIM)
            total = dot_nt(ones, high[:, part]) + dot_nt(ones, rest_of[:, part])
            at = n * TILE + i * HEAD_DIM
            t, g, inside = at // SHARD, at % SHARD // per, at % per
            to = t * per + inside
            g_parts[g][:, to : to + HEAD_DIM] = grad[:, part]
            h = to // HEAD_DIM
            deltas[g][h : h + 1, :] = total[:1]
    out_copy.wait()
    resid_copy.wait()
    grads_stored(keep, send, grad_sems)


def feed_forward(meta, inner, inputs, dout, bo, gain, shift, bup, bdn, parts, pieces):
    tokens, width = inputs.shape
    groups = len(parts)
    half = max(inner // 2, 1)
    travel = ((half, width // SHARD, 3, width // inner, SHARD), BF16)
    wide = pltpu.VMEM((tokens, width), F32)
    slim = pltpu.VMEM((tokens, width), BF16)
    return call(
        functools.partial(feed_kernel, len(pieces), groups),
        [(parts[0].shape, BF16)] * groups
        + [((width // HEAD_DIM // groups, tokens), F32)] * groups
        + [((8, width), F32), ((tokens, width), BF16), ((tokens, width), F32), travel, travel],
        [meta, inputs, dout, bo, gain, shift, bup, bdn, *parts, *pieces],
        [
            pltpu.VMEM((3, width, width), BF16),
            slim,
            wide,
            wide,
            pltpu.VMEM((tokens, 128), F32),
            slim,
            slim,
            slim,
            wide,
            slim,
            slim,
            pltpu.VMEM((3, width, width), BF16),
            pltpu.SemaphoreType.DMA,
            pltpu.SemaphoreType.DMA((2,)),
            pltpu.SemaphoreType.DMA((2,)),
        ],
        "feed_forward",
        smem=1,
        anys=len(pieces),
        out_anys=4,
    )


def backward_kernel(n_pieces, off, more, meta, rng, segq, segk, lse, delta, q, do, k, v, *refs):
    if more:
        left_in, right_in, *refs = refs
    low_in, *refs = refs
    shards, pieces, refs = refs[:3], refs[3 : 3 + n_pieces], refs[3 + n_pieces :]
    left, own, right, sums, keep, send, *refs = refs
    low, w, dq, dk, dv, dk_acc, dv_acc, dq_acc, grads, sem, low_sem, grad_sems = refs
    low_copy = pltpu.make_async_copy(low_in, low, low_sem)
    low_copy.start()
    wait = load_weights(meta, shards, off, pieces, w, sem)
    tokens, width = q.shape
    start, stop = tokens - FAR, 2 * tokens + FAR
    near, middle = slice(start, stop), slice(tokens, 2 * tokens)
    before, after = used_chunks(rng)
    scale = HEAD_DIM**-0.5

    def zero(rows):
        dk_acc[rows, :] = jnp.zeros((rows.stop - rows.start, width), F32)
        dv_acc[rows, :] = jnp.zeros((rows.stop - rows.start, width), F32)

    def narrow(rows):
        dk[rows, :] = (dk_acc[rows, :] * scale).astype(BF16)
        dv[rows, :] = dv_acc[rows, :].astype(BF16)

    def ends(act):
        pl.when(before)(lambda: act(slice(0, start)))
        pl.when(after)(lambda: act(slice(stop, 3 * tokens)))

    zero(near)
    ends(zero)
    attend_back(rng, segq, segk, lse, delta, q, do, k, v, dq, dk_acc, dv_acc, dq_acc)
    narrow(near)
    ends(narrow)

    low_copy.wait()
    grads[0] = dot_tn(low[middle, :], dq[...]).astype(BF16)
    sums[...] = jnp.zeros(sums.shape, F32)
    sums[0:1, :] = jnp.sum(dq[...].astype(F32), axis=0, keepdims=True)

    sums[1:2, :] = jnp.sum(dv[near, :].astype(F32), axis=0, keepdims=True)
    grads[1] = dot_tn(low[near, :], dk[near, :]).astype(BF16)
    grads[2] = dot_tn(low[near, :], dv[near, :]).astype(BF16)

    for i, used in enumerate((before, after)):

        @pl.when(used)
        def _():
            rows = slice(i * stop, i * stop + start)
            sums[1:2, :] += jnp.sum(dv[rows, :].astype(F32), axis=0, keepdims=True)
            for m, x in ((1, dk), (2, dv)):
                more = dot_tn(low[rows, :], x[rows, :])
                grads[m] = (grads[m].astype(F32) + more).astype(BF16)

    store_grads(meta, grads, keep, send, grad_sems, 0, 3)

    wait()

    def halo_grads(out, old, to, rows):
        res = dot_nt(dk[rows, :], w[1]) + dot_nt(dv[rows, :], w[2])
        if more:
            res = res + old[to, :].astype(F32)
        out[to, :] = res.astype(BF16)

    lows, highs = slice(0, tokens - FAR), slice(tokens - FAR, tokens)
    firsts, others = slice(0, FAR), slice(FAR, tokens)
    for out, old, used, far_to, near_to, base in (
        (left, left_in if more else None, before, lows, highs, 0),
        (right, right_in if more else None, after, others, firsts, 2 * tokens),
    ):
        halo_grads(out, old, near_to, slice(base + near_to.start, base + near_to.stop))

        @pl.when(used)
        def _():
            halo_grads(out, old, far_to, slice(base + far_to.start, base + far_to.stop))

        @pl.when(jnp.logical_not(used))
        def _():
            if more:
                out[far_to, :] = old[far_to, :]
            else:
                out[far_to, :] = jnp.zeros((tokens - FAR, out.shape[1]), BF16)

    own[...] = (
        dot_nt(dk[middle, :], w[1]) + dot_nt(dv[middle, :], w[2]) + dot_nt(dq[...], w[0])
    )
    grads_stored(keep, send, grad_sems)


def backward(group, meta, rng, segq, segk, lse, delta, q, do, k, v, old, low, shards, pieces):
    tokens, cols = q.shape
    width = low.shape[1]
    window = 3 * tokens
    per = pieces[0].shape[3]
    travel = ((max(len(pieces) // 2, 1), cols // per, *pieces[0].shape[1:]), BF16)
    slim, wide, full = (tokens, cols), (window, cols), (tokens, width)
    return call(
        functools.partial(backward_kernel, len(pieces), group * per, len(old) > 0),
        [(full, BF16), (full, F32), (full, BF16), ((8, cols), F32), travel, travel],
        [meta, rng, segq, segk, lse, delta, q, do, k, v, *old, low, *shards, *pieces],
        [
            pltpu.VMEM((window, width), BF16),
            pltpu.VMEM((3, width, cols), BF16),
            pltpu.VMEM(slim, BF16),
            pltpu.VMEM(wide, BF16),
            pltpu.VMEM(wide, BF16),
            pltpu.VMEM(wide, F32),
            pltpu.VMEM(wide, F32),
            pltpu.VMEM((cols // HEAD_DIM, HEAD_DIM, BLOCK), F32),
            pltpu.VMEM((3, width, cols), BF16),
            pltpu.SemaphoreType.DMA,
            pltpu.SemaphoreType.DMA,
            pltpu.SemaphoreType.DMA((2,)),
        ],
        "backward_attention",
        smem=2,
        anys=4 + len(pieces),
        out_anys=2,
    )


def last_kernel(inputs, g_resid, from_left, from_right, gain, *refs):
    *owns, g_inputs, sums = refs
    sums[...] = jnp.zeros(sums.shape, F32)

    @pl.loop(0, inputs.shape[0] // ROWS)
    def _(i):
        rows = pl.ds(pl.multiple_of(i * ROWS, ROWS), ROWS)
        hat, rstd = normalise(inputs[rows, :].astype(F32))
        g = from_left[rows, :].astype(F32) + from_right[rows, :].astype(F32)
        for own in owns:
            g = g + own[rows, :]
        g_inputs[rows, :] = (g_resid[rows, :] + norm_back(g, hat, rstd, gain[...])).astype(BF16)
        sums[0:1, :] += jnp.sum(g * hat, axis=0, keepdims=True)
        sums[1:2, :] += jnp.sum(g, axis=0, keepdims=True)


def last_step(inputs, g_resid, from_left, from_right, gain, owns):
    return call(
        last_kernel,
        [(inputs.shape, BF16), ((8, inputs.shape[1]), F32)],
        [inputs, g_resid, from_left, from_right, gain, *owns],
        [],
        "input_norm_grads",
    )


def lay_out_kernel(turned, groups, meta, *refs):
    outs = refs[-len(turned) :]
    pieces = refs[: -len(turned)]
    n = len(pieces) // groups
    s = meta[0]
    size, per = pieces[0].shape[-2:]
    for g in range(groups):
        to = slice(g * per, (g + 1) * per)
        if n == 1:
            whole = [
                (pieces[g].at[i], slice(i * size, (i + 1) * size))
                for i in range(pieces[g].shape[0])
            ]
        else:
            whole = [
                (pieces[g * n + j], pl.ds(pl.multiple_of((s ^ j) * size, size), size))
                for j in range(n)
            ]
        for piece, at in whole:
            for m, turn in enumerate(turned):
                if turn:
                    outs[m][to, at] = jnp.transpose(piece[m].astype(F32))
                else:
                    outs[m][at, to] = piece[m].astype(F32)


def lay_out(meta, groups, turned):
    first = groups[0]
    width = first[0].shape[-2] * (len(first) if len(first) > 1 else first[0].shape[0])
    shapes = [(SHARD, width) if turn else (width, SHARD) for turn in turned]
    return call(
        functools.partial(lay_out_kernel, turned, len(groups)),
        [(shape, F32) for shape in shapes],
        [meta, *[piece for group in groups for piece in group]],
        [],
        "lay_out_grads",
        smem=1,
    )


SHARD = 256


def make_body(n_seq, n_tp):
    inner = min(n_seq, 8)
    outer = n_seq // inner
    half = inner // 2
    masks = [2 * jj for jj in range(1, half)]

    def shift(x, by):
        pairs = [(i, i + by) for i in range(n_tp) if 0 <= i + by < n_tp]
        return lax.ppermute(x, "tp", pairs)

    def swap(x, mask):
        return lax.ppermute(x, "seq", [(i, i ^ mask) for i in range(n_seq)])

    def tie(*xs):
        return lax.optimization_barrier(xs)

    def over_tp(shards, biases, off, per, s, t, after):
        size = shards[0].shape[0] // inner
        cut = jnp.stack([lax.dynamic_slice(w, (s * size, off), (size, per)) for w in shards])
        parts = []
        rest = jnp.stack([b[off : off + per] for b in biases])
        for _ in range(3):
            part = rest.astype(BF16)
            rest = rest - part.astype(F32)
            parts.append(part)
        parts = jnp.stack(parts + [jnp.zeros_like(parts[0])] * 13, axis=1)
        block = jnp.concatenate([cut, parts], axis=1)
        block = jnp.broadcast_to(block[None], (n_tp, *block.shape))
        if after is not None:
            block, _ = tie(block, after)
        got = lax.all_to_all(block, "tp", 0, 0, tiled=True)
        others = jnp.stack(
            [lax.dynamic_index_in_dim(got, lax.rem(t + r + 1, n_tp), 0, keepdims=False)[:, :size]
             for r in range(n_tp - 1)]
        )
        whole = jnp.sum(got[:, :, size : size + 3].astype(F32), axis=2)
        whole = [whole[:, m].reshape(1, n_tp * per) for m in range(len(biases))]
        return others, whole, got

    def from_chips(x):
        return [x] + [swap(x, mask) for mask in masks]

    def from_cores(even):
        odd = [swap(e, 1) for e in even]
        return [e for pair in zip(even, odd) for e in pair]

    def over_cores(keep, send):
        got = swap(send, 1)
        return [(keep[jj].astype(F32) + got[jj].astype(F32)).astype(BF16) for jj in range(half)]

    def over_chips(sums):
        moved = [swap(sums[jj], 2 * jj) for jj in range(1, half)]
        total = sums[0].astype(F32)
        for x in moved:
            total = total + x.astype(F32)
        total = total.astype(BF16)
        if outer > 1:
            groups = [[i + inner * o for o in range(outer)] for i in range(inner)]
            total = lax.psum(total, "seq", axis_index_groups=groups)
        return total

    def own_shard(total):
        got = lax.all_to_all(total, "tp", 0, 0, tiled=True)
        return jnp.sum(got.astype(F32), axis=0).astype(BF16)

    def body(
        inputs, segment_ids, row_lengths, norm1_gain, norm1_shift, w_query, w_key, w_value,
        b_query, b_value, w_out, b_out, norm2_gain, norm2_shift, w_up, b_up, w_down, b_down,
        out_grad,
    ):
        tokens, width = inputs.shape
        halo = tokens
        t = lax.axis_index("tp")
        s = lax.rem(lax.axis_index("seq"), inner)
        meta = jnp.stack([s, t]).astype(jnp.int32)
        per = SHARD // GROUPS
        every = range(GROUPS)
        zero = jnp.zeros_like(b_query)

        def row(x):
            return x.reshape(1, -1)

        def by_shard(groups):
            cols = [x.reshape(n_tp, per) for x in groups]
            return jnp.concatenate(cols, axis=1).reshape(1, width)

        attn_w = [w_query, w_key, w_value]
        attn_b = [b_query, b_up, b_value]
        done, dones = None, []
        attn_p, attn_whole = [], []
        for g in every:
            others, whole, done = over_tp(attn_w, attn_b, g * per, per, s, t, done)
            dones.append(done)
            even = from_chips(others)
            even[0], _ = tie(even[0], even[-1])
            attn_p.append(from_cores(even))
            attn_whole.append(whole)
        feed_w = [w_out.T, w_up, w_down.T]
        size = width // n_seq
        at = lax.axis_index("seq") * size
        cut = jnp.stack([lax.dynamic_slice_in_dim(w, at, size, 0) for w in feed_w])
        feed_p = [lax.all_gather(cut, ("seq", "tp"), axis=0)]
        inputs_later, _ = tie(inputs, dones[0])
        left = shift(inputs_later, 1)
        right = shift(inputs_later, -1)

        position = jnp.arange(ROW_LEN, dtype=jnp.int32)
        numbers = jnp.where(position < row_lengths[0], segment_ids[0], 4096 + position)
        numbers = jnp.concatenate(
            [jnp.full((halo,), -1, jnp.int32), numbers, jnp.full((halo,), 1 << 20, jnp.int32)]
        )
        seg_win = lax.dynamic_slice_in_dim(numbers, t * tokens, tokens + 2 * halo, 0)
        seg_mine = seg_win[halo : halo + tokens]
        first = seg_mine[::BLOCK]
        last = seg_mine[BLOCK - 1 :: BLOCK]
        low = jnp.sum((seg_win[None, :] < first[:, None]).astype(jnp.int32), axis=1)
        high = jnp.sum((seg_win[None, :] <= last[:, None]).astype(jnp.int32), axis=1)
        rng = jnp.stack([low // BLOCK, (high + BLOCK - 1) // BLOCK])
        segq, segk = seg_mine[None, :], seg_win[:, None]

        source = (row(norm1_gain), row(norm1_shift), left, inputs, right)
        saved = []
        for g in every:
            bq, _, bv = attn_whole[g]
            res = forward(g, meta, rng, segq, segk, source, bq, bv, attn_w, attn_p[g])
            mixed, lse, q, k, v = res[:5]
            if g == 0:
                source = first_low = res[5]
            saved.append((mixed, lse, q, k, v))
        bup = by_shard([x[1] for x in attn_whole])
        res = feed_forward(
            meta, inner, inputs, out_grad, row(b_out), row(norm2_gain), row(norm2_shift), bup,
            row(b_down), [x[0] for x in saved], feed_p,
        )
        g_mixed, delta = list(res[:GROUPS]), res[GROUPS : 2 * GROUPS]
        sums_feed, output, g_resid, keep, send = res[2 * GROUPS :]

        sums = over_cores(keep, send)
        g_mixed[0], *sums = tie(g_mixed[0], *sums)
        feed_total = over_chips(sums)
        old, owns, sums_qkv, totals = (), [], [], []
        for g in every:
            _, lse, q, k, v = saved[g]
            dx_left, own, dx_right, vec, keep, send = backward(
                g, meta, rng, segq, segk, lse, delta[g], q, g_mixed[g], k, v, old,
                first_low, attn_w, attn_p[g],
            )
            old = (dx_left, dx_right)
            owns.append(own)
            sums_qkv.append(vec)
            if g > 0:
                send, totals[g - 1] = tie(send, totals[g - 1])
            else:
                send, feed_total = tie(send, feed_total)
            sums = over_cores(keep, send)
            if g + 1 < GROUPS:
                g_mixed[g + 1], *sums = tie(g_mixed[g + 1], *sums)
            else:
                owns[g], *sums = tie(owns[g], *sums)
            totals.append(over_chips(sums))
        from_right = shift(dx_left, -1)
        from_left = shift(dx_right, 1)
        piece = feed_total.shape[1:]
        feed_g = feed_total.reshape(-1, SHARD)
        feed_g = lax.psum_scatter(feed_g, "tp", scatter_dimension=0, tiled=True)
        shards = []
        for g in every:
            shards.append(own_shard(totals[g]))
        g_inputs, sums_in = last_step(
            inputs, g_resid, from_left, from_right, row(norm1_gain), owns
        )

        g_inputs, feed_g = tie(g_inputs, feed_g)
        feed_g = lax.all_gather(feed_g.reshape(piece), "seq", axis=0)[:inner]
        vectors = [by_shard([x[i] for x in sums_qkv]) for i in range(2)]
        vectors = [sums_in[:2], *vectors, sums_feed[:5]]
        vectors = jnp.concatenate(vectors)
        n_vec = vectors.shape[0]
        vectors, shards[-1] = tie(vectors, shards[-1])
        vectors = vectors.reshape(n_seq * n_tp, -1)
        vectors = lax.all_to_all(vectors, ("seq", "tp"), 0, 0, tiled=True)
        vectors = jnp.broadcast_to(jnp.sum(vectors, axis=0, keepdims=True), vectors.shape)
        vectors = lax.all_to_all(vectors, ("seq", "tp"), 0, 0, tiled=True)
        vectors = vectors.reshape(n_vec, width)
        n1g, n1s, g_bq, g_bv, g_bo, n2g, n2s, g_bup, g_bdn = [vectors[i] for i in range(9)]

        pieces = [from_cores(from_chips(x)) for x in shards]
        g_wq, g_wk, g_wv = lay_out(meta, pieces, (False, False, False))
        g_wo, g_wup, g_wdn = lay_out(meta, [[feed_g]], (True, False, True))

        def shard(x):
            return lax.dynamic_slice_in_dim(x, t * SHARD, SHARD, 0)

        return (
            output, g_inputs, n1g, n1s, g_wq, g_wk, g_wv, shard(g_bq), shard(g_bv),
            g_wo, g_bo, n2g, n2s, g_wup, shard(g_bup), g_wdn, g_bdn,
        )

    return body


def solution(mesh):
    tok = P(("seq", "tp"), None)
    col, row, vec, rep = P(None, "tp"), P("tp", None), P("tp"), P()
    in_specs = (
        tok, P("seq", None), P("seq"), rep, rep, col, col, col, vec, vec,
        row, rep, rep, rep, col, vec, row, rep, tok,
    )
    out_specs = (
        tok, tok, rep, rep, col, col, col, vec, vec,
        row, rep, rep, rep, col, vec, row, rep,
    )
    body = make_body(mesh.shape["seq"], mesh.shape["tp"])
    return jax.shard_map(body, mesh=mesh, in_specs=in_specs, out_specs=out_specs, check_vma=False)
```

profile of v0, /device:TPU:0, one launch (start us, length us, event | category | flops | bytes accessed | tf_op | source)
XLA Modules:
  0.0 312.3 jit_solution(9258797482427533138)
XLA Ops:
  7.3 0.9 constant_dynamic-slice_fusion.3
  8.5 0.7 pad_maximum_fusion.2
  9.2 0.7 subtract_convert_fusion
  9.9 0.8 dynamic-slice_bitcast_fusion.6
  10.8 0.9 dynamic-slice_bitcast_fusion.4
  11.9 1.0 broadcast_in_dim.12
  12.9 6.3 %all-to-all-start = ((bf16[4,3,144,256]{3,2,1,0:T(8,128)(2,1)}), bf16[4,3,144,256]{3,2,1,0:T(8,128)(2,1)S(1)}, u32[]{:S(2)}, u32[]{:S(2)}) async-start(bf16[4,3,144,256]{3,2,1,0:T(8,128)(2,1)} %broadcast_in_dim.12), calls=%async_computation | async-start | bytes 1769472 | tf_op jit(solution)/shard_map/all_to_all | solution.py:650
  19.2 26.4 %all-to-all-done = bf16[4,3,144,256]{3,2,1,0:T(8,128)(2,1)S(1)} async-done(((bf16[4,3,144,256]{3,2,1,0:T(8,128)(2,1)}), bf16[4,3,144,256]{3,2,1,0:T(8,128)(2,1)S(1)}, u32[]{:S(2)}, u32[]{:S(2)}) %all-to-all-start) | async-done | bytes 884768 | tf_op jit(solution)/shard_map/all_to_all | solution.py:650
  45.6 2.3 collective-permute-start
  48.1 2.5 collective-permute-start.2
  50.6 0.5 collective-permute-start.4
  52.3 1.3 collective-permute-start.1
  54.2 15.6 %collective-permute-done.2.refs_16_.refs_10_ = bf16[3,3,128,256]{3,2,1,0:T(8,128)(2,1)S(1)} collective-permute-done((bf16[3,3,128,256]{3,2,1,0:T(8,128)(2,1)S(1)}, bf16[3,3,128,256]{3,2,1,0:T(8,128)(2,1)S(1)}, u32[]{:S(2)}, u32[]{:S(2)}) %collective-permute-start.2) | collective-permute-done | bytes 589856 | tf_op jit(solution)/shard_map/ppermute | solution.py:631
  69.8 14.6 %collective-permute-done.4.refs_12_.refs_6_ = bf16[3,3,128,256]{3,2,1,0:T(8,128)(2,1)} collective-permute-done((bf16[3,3,128,256]{3,2,1,0:T(8,128)(2,1)S(1)}, bf16[3,3,128,256]{3,2,1,0:T(8,128)(2,1)}, u32[]{:S(2)}, u32[]{:S(2)}) %collective-permute-start.4) | collective-permute-done | bytes 589856 | tf_op jit(solution)/shard_map/ppermute | solution.py:631
  85.0 1.1 broadcast_in_dim.34.segk
  86.1 0.6 pad_add_fusion.1.meta
  86.7 0.6 pad_add_fusion.rng
  87.3 0.6 fusion.14
  87.9 7.0 %collective-permute-done.1.refs_6_ = bf16[512,1024]{1,0:T(8,128)(2,1)} collective-permute-done((bf16[512,1024]{1,0:T(8,128)(2,1)S(1)}, bf16[512,1024]{1,0:T(8,128)(2,1)}, u32[]{:S(2)}, u32[]{:S(2)}) %collective-permute-start.1) | collective-permute-done | bytes 1048608 | tf_op jit(solution)/shard_map/ppermute | solution.py:628
  95.1 0.7 copy-done.10
  96.4 17.5 %forward_attention.1 = (bf16[512,1024]{1,0:T(8,128)(2,1)}, f32[8,512]{1,0:T(8,128)}, bf16[512,1024]{1,0:T(8,128)(2,1)}, bf16[1536,1024]{1,0:T(8,128)(2,1)}, bf16...) custom-call(s32[2]{0:T(128)} %pad_add_fusion.1.meta, s32[2,2]{1,0:T(2,128)} %pad_add_fusion.rng, s32[1,512]{1,0:T(1,128)} %bitcast.104, ...), custom_call_target="tpu_custom_call" | custom-call | flops 49999998976 | bytes 1000000 | tf_op jit(solution)/shard_map/forward_attention/pallas_call | solution.py:54
  113.9 21.9 %feed_forward.1 = (bf16[512,1024]{1,0:T(8,128)(2,1)}, f32[8,512]{1,0:T(8,128)}, f32[8,1024]{1,0:T(8,128)}, bf16[512,1024]{1,0:T(8,128)(2,1)}, f32[512,1024]{1,0:...) custom-call(s32[2]{0:T(128)} %pad_add_fusion.1.meta, bf16[512,1024]{1,0:T(8,128)(2,1)} %inputs.3, ...), custom_call_target="tpu_custom_call" | custom-call | flops 49999998976 | bytes 1000000 | tf_op jit(solution)/shard_map/feed_forward/pallas_call | solution.py:54
  135.9 5.9 %collective-permute-done.9 = bf16[4,4,3,128,256]{4,3,2,1,0:T(8,128)(2,1)S(1)} collective-permute-done((bf16[4,4,3,128,256]{4,3,2,1,0:T(8,128)(2,1)}, bf16[4,4,3,128,256]{4,3,2,1,0:T(8,128)(2,1)S(1)}, u32[]{:S(2)}, u32[]{:S(2)}) %collective-permute-start.9) | collective-permute-done | bytes 3145760 | tf_op jit(solution)/shard_map/ppermute | solution.py:631
  141.7 3.0 fusion.3
  144.7 2.5 collective-permute-start.12
  147.2 1.3 collective-permute-start.13
  148.5 1.4 collective-permute-start.14
  149.9 26.3 %backward_attention.1 = (bf16[512,1024]{1,0:T(8,128)(2,1)}, f32[512,1024]{1,0:T(8,128)}, bf16[512,1024]{1,0:T(8,128)(2,1)}, f32[8,1024]{1,0:T(8,128)}, bf16[4,4,...) custom-call(s32[2]{0:T(128)} %pad_add_fusion.1.meta, s32[2,2]{1,0:T(2,128)} %pad_add_fusion.rng, ...), custom_call_target="tpu_custom_call" | custom-call | flops 49999998976 | bytes 1000000 | tf_op jit(solution)/shard_map/backward_attention/pallas_call | solution.py:54
  176.2 6.2 %collective-permute-done.13 = bf16[4,3,128,256]{3,2,1,0:T(8,128)(2,1)S(1)} collective-permute-done((bf16[4,3,128,256]{3,2,1,0:T(8,128)(2,1)S(1)}, bf16[4,3,128,256]{3,2,1,0:T(8,128)(2,1)S(1)}, u32[]{:S(2)}, u32[]{:S(2)}) %collective-permute-start.13) | collective-permute-done | bytes 786464 | tf_op jit(solution)/shard_map/ppermute | solution.py:631
  182.5 1.8 collective-permute-done.14
  184.3 1.3 add_convert_fusion.5
  185.6 5.9 %collective-permute-done.15 = bf16[4,4,3,128,256]{4,3,2,1,0:T(8,128)(2,1)S(1)} collective-permute-done((bf16[4,4,3,128,256]{4,3,2,1,0:T(8,128)(2,1)}, bf16[4,4,3,128,256]{4,3,2,1,0:T(8,128)(2,1)S(1)}, u32[]{:S(2)}, u32[]{:S(2)}) %collective-permute-start.15) | collective-permute-done | bytes 3145760 | tf_op jit(solution)/shard_map/ppermute | solution.py:631
  191.5 1.4 fusion.7
  192.9 0.6 collective-permute-start.16
  193.5 1.7 collective-permute-start.17
  195.3 1.2 collective-permute-start.18
  196.4 5.7 %collective-permute-start.10 = (bf16[512,1024]{1,0:T(8,128)(2,1)}, bf16[512,1024]{1,0:T(8,128)(2,1)}, u32[]{:S(2)}, u32[]{:S(2)}) collective-permute-start(bf16[512,1024]{1,0:T(8,128)(2,1)} %get-tuple-element.77), channel_id=1, source_target_pairs={{0,1},{1,2},{2,3},{4,5},{5,6},{6,7},{8,9},{9,10},{10,11},{12,13},{... | collective-permute-start | bytes 3145736 | tf_op jit(solution)/shard_map/ppermute | solution.py:628
  202.1 1.3 collective-permute-start.11
  203.4 0.8 slice.143
  204.2 9.2 %collective-permute-done.16 = bf16[4,3,128,256]{3,2,1,0:T(8,128)(2,1)} collective-permute-done((bf16[4,3,128,256]{3,2,1,0:T(8,128)(2,1)S(1)}, bf16[4,3,128,256]{3,2,1,0:T(8,128)(2,1)}, u32[]{:S(2)}, u32[]{:S(2)}) %collective-permute-start.16) | collective-permute-done | bytes 786464 | tf_op jit(solution)/shard_map/ppermute | solution.py:631
  213.4 16.3 %collective-permute-done.17 = bf16[4,3,128,256]{3,2,1,0:T(8,128)(2,1)} collective-permute-done((bf16[4,3,128,256]{3,2,1,0:T(8,128)(2,1)S(1)}, bf16[4,3,128,256]{3,2,1,0:T(8,128)(2,1)}, u32[]{:S(2)}, u32[]{:S(2)}) %collective-permute-start.17) | collective-permute-done | bytes 786464 | tf_op jit(solution)/shard_map/ppermute | solution.py:631
  229.8 2.9 add_convert_fusion
  232.7 5.7 %all-to-all-start.1 = ((bf16[4,3,128,256]{3,2,1,0:T(8,128)(2,1)}), bf16[4,3,128,256]{3,2,1,0:T(8,128)(2,1)S(1)}, u32[]{:S(2)}, u32[]{:S(2)}) async-start(bf16[4,3,128,256]{3,2,1,0:T(8,128)(2,1)} %add_convert_fusion), calls=%async_computation.2 | async-start | bytes 1572864 | tf_op jit(solution)/shard_map/all_to_all | solution.py:682
  238.4 3.6 %collective-permute-done.11.from_right = bf16[512,1024]{1,0:T(8,128)(2,1)} collective-permute-done((bf16[512,1024]{1,0:T(8,128)(2,1)}, bf16[512,1024]{1,0:T(8,128)(2,1)}, u32[]{:S(2)}, u32[]{:S(2)}) %collective-permute-start.11) | collective-permute-done | bytes 1048608 | tf_op jit(solution)/shard_map/ppermute | solution.py:628
  242.0 6.2 %input_norm_grads.1 = (bf16[512,1024]{1,0:T(8,128)(2,1)}, f32[8,1024]{1,0:T(8,128)}) custom-call(bf16[512,1024]{1,0:T(8,128)(2,1)} %inputs.3, f32[512,1024]{1,0:T(8,128)} %get-tuple-element.66.g_resid, bf16[512,1024]{1,0:T(8,128)(2,1)} %collective-permute-done.10.from_left, bf16[512,1024]{1,0:T(8,128)(2,1)} %collective-permute-done.11.from_right, ...), custom_call_target="tpu_custom_call" | custom-call | flops 49999998976 | bytes 1000000 | tf_op jit(solution)/shard_map/input_norm_grads/pallas_call | solution.py:54
  248.2 0.8 slice.142
  249.0 8.9 %all-to-all-done.1 = bf16[4,3,128,256]{3,2,1,0:T(8,128)(2,1)S(1)} async-done(((bf16[4,3,128,256]{3,2,1,0:T(8,128)(2,1)}), bf16[4,3,128,256]{3,2,1,0:T(8,128)(2,1)S(1)}, u32[]{:S(2)}, u32[]{:S(2)}) %all-to-all-start.1) | async-done | bytes 786464 | tf_op jit(solution)/shard_map/all_to_all | solution.py:682
  258.2 10.7 %all_to_all.26 = f32[32,1,288]{2,1,0:T(1,128)S(1)} all-to-all(f32[32,1,288]{2,1,0:T(1,128)S(1)} %all_to_all.21), channel_id=1, replica_groups=mesh['seq'=8,'tp'=4] {'seq','tp'}, dimensions={0} | all-to-all | bytes 73728 | tf_op jit(solution)/shard_map/all_to_all | solution.py:800
  269.0 0.6 broadcast_in_dim.33
  269.6 2.6 all-to-all-start.3
  272.3 0.7 all-gather.4.cloned.1.call-update
  272.9 1.7 collective-permute-start.20
  274.6 1.5 collective-permute-start.22
  276.5 3.1 all-to-all-done.3
  279.8 0.6 fusion.13
  280.5 0.6 constant_dynamic-slice_fusion.2
  281.0 4.8 %collective-permute-done.22.refs_4_ = bf16[3,128,256]{2,1,0:T(8,128)(2,1)S(1)} collective-permute-done((bf16[3,128,256]{2,1,0:T(8,128)(2,1)S(1)}, bf16[3,128,256]{2,1,0:T(8,128)(2,1)S(1)}, u32[]{:S(2)}, u32[]{:S(2)}) %collective-permute-start.22) | collective-permute-done | bytes 196640 | tf_op jit(solution)/shard_map/ppermute | solution.py:631
  286.3 0.6 constant_dynamic-slice_fusion.1
  286.9 0.6 constant_dynamic-slice_fusion
  287.5 0.6 copy-done.17
  288.3 0.7 copy-done.20
  288.9 3.3 %lay_out_grads.2 = (f32[1024,256]{1,0:T(8,128)}, f32[1024,256]{1,0:T(8,128)}, f32[1024,256]{1,0:T(8,128)}) custom-call(s32[2]{0:T(128)} %pad_add_fusion.1.meta, bf16[3,128,256]{2,1,0:T(8,128)(2,1)} %copy-done.4, bf16[3,128,256]{2,1,0:T(8,128)(2,1)} %copy-done.17, bf16[3,128,256]{2,1,0:T(8,128)(2,1)} %copy-done.14, bf16[3,128,256]{2,1,0:T(8,128)(2,1)} %copy-done.18, ...), custom_call_target="tpu_custom_call" | custom-call | flops 49999998976 | bytes 1000000 | tf_op jit(solution)/shard_map/lay_out_grads/pallas_call | solution.py:54
  292.3 9.6 %all-gather.4.cloned.1.call-done.refs_0_ = bf16[8,3,128,256]{3,2,1,0:T(8,128)(2,1)} async-done(((bf16[1,3,128,256]{3,2,1,0:T(8,128)(2,1)}), bf16[8,3,128,256]{3,2,1,0:T(8,128)(2,1)}) %all-gather.4.cloned.1.call-update) | async-done | bytes 1572880 | tf_op jit(solution)/shard_map/all_gather | solution.py:793
  301.9 3.6 %lay_out_grads.3 = (f32[256,1024]{1,0:T(8,128)}, f32[1024,256]{1,0:T(8,128)}, f32[256,1024]{1,0:T(8,128)}) custom-call(s32[2]{0:T(128)} %pad_add_fusion.1.meta, bf16[8,3,128,256]{3,2,1,0:T(8,128)(2,1)} %all-gather.4.cloned.1.call-done.refs_0_), custom_call_target="tpu_custom_call" | custom-call | flops 49999998976 | bytes 1000000 | tf_op jit(solution)/shard_map/lay_out_grads/pallas_call | solution.py:54
  (103 shorter events, 4.8 us)
Async XLA Ops:
  7.2 1.2 copy-start
  7.2 106.7 %all-gather.6.cloned.1.call-start = ((), (), s32[]{:S(2)}) async-start(), calls=%async_computation.7 | async-start | bytes 6488064 | tf_op jit(solution)/shard_map/all_gather | solution.py:721
  11.9 33.7 %copy-start.8 = (bf16[512,1024]{1,0:T(8,128)(2,1)S(1)}, bf16[512,1024]{1,0:T(8,128)(2,1)}, u32[]{:S(2)}) copy-start(bf16[512,1024]{1,0:T(8,128)(2,1)} %inputs.3) | copy-start | bytes 3145732
  12.9 32.7 %all-to-all-start = ((bf16[4,3,144,256]{3,2,1,0:T(8,128)(2,1)}), bf16[4,3,144,256]{3,2,1,0:T(8,128)(2,1)S(1)}, u32[]{:S(2)}, u32[]{:S(2)}) async-start(bf16[4,3,144,256]{3,2,1,0:T(8,128)(2,1)} %broadcast_in_dim.12), calls=%async_computation | async-start | bytes 1769472 | tf_op jit(solution)/shard_map/all_to_all | solution.py:650
  19.2 253.1 %reduce-scatter.2.cloned.1.call-start = ((), (), s32[]{:S(2)}) async-start(), calls=%async_computation.5 | async-start | bytes 983040 | tf_op jit(solution)/shard_map/reduce_scatter | solution.py:784
  19.2 34.4 %copy-start.6 = (s32[1,2048]{1,0:T(1,128)S(1)}, s32[1,2048]{1,0:T(1,128)}, u32[]{:S(2)}) copy-start(s32[1,2048]{1,0:T(1,128)} %param.20) | copy-start | bytes 24580
  45.6 39.2 %collective-permute-start = (bf16[512,1024]{1,0:T(8,128)(2,1)S(1)}, bf16[512,1024]{1,0:T(8,128)(2,1)}, u32[]{:S(2)}, u32[]{:S(2)}) collective-permute-start(bf16[512,1024]{1,0:T(8,128)(2,1)S(1)} %copy-done.8), channel_id=1, source_target_pairs={{0,1},{1,2},{2,3},{4,5},{5,6},{6,7},{8,9},{9,10},{10,11},{12,13},{... | collective-permute-start | bytes 3145736 | tf_op jit(solution)/shard_map/ppermute | solution.py:628
  48.1 47.0 %copy-start.3 = (bf16[3,3,128,256]{3,2,1,0:T(8,128)(2,1)}, bf16[3,3,128,256]{3,2,1,0:T(8,128)(2,1)S(1)}, u32[]{:S(2)}) copy-start(bf16[3,3,128,256]{3,2,1,0:T(8,128)(2,1)S(1)} %pad_maximum_fusion.refs_10_.refs_4_) | copy-start | bytes 1769476
  48.1 21.6 %collective-permute-start.2 = (bf16[3,3,128,256]{3,2,1,0:T(8,128)(2,1)S(1)}, bf16[3,3,128,256]{3,2,1,0:T(8,128)(2,1)S(1)}, u32[]{:S(2)}, u32[]{:S(2)}) collective-permute-start(bf16[3,3,128,256]{3,2,1,0:T(8,128)(2,1)S(1)} %pad_maximum_fusion.refs_10_.refs_4_), channel_id=1, source_target_pairs={{0,24},{4,28},{8,16},{12,20},{16,8},{20,12},{24,0},{28,4},{1,25},{... | collective-permute-start | bytes 1769480 | tf_op jit(solution)/shard_map/ppermute | solution.py:631
  50.6 33.7 %collective-permute-start.4 = (bf16[3,3,128,256]{3,2,1,0:T(8,128)(2,1)S(1)}, bf16[3,3,128,256]{3,2,1,0:T(8,128)(2,1)}, u32[]{:S(2)}, u32[]{:S(2)}) collective-permute-start(bf16[3,3,128,256]{3,2,1,0:T(8,128)(2,1)S(1)} %pad_maximum_fusion.refs_10_.refs_4_), channel_id=1, source_target_pairs={{0,8},{4,12},{8,0},{12,4},{16,24},{20,28},{24,16},{28,20},{1,9},{5... | collective-permute-start | bytes 1769480 | tf_op jit(solution)/shard_map/ppermute | solution.py:631
  51.2 33.2 %collective-permute-start.6 = (bf16[3,3,128,256]{3,2,1,0:T(8,128)(2,1)S(1)}, bf16[3,3,128,256]{3,2,1,0:T(8,128)(2,1)}, u32[]{:S(2)}, u32[]{:S(2)}) collective-permute-start(bf16[3,3,128,256]{3,2,1,0:T(8,128)(2,1)S(1)} %pad_maximum_fusion.refs_10_.refs_4_), channel_id=1, source_target_pairs={{0,16},{4,20},{8,24},{12,28},{16,0},{20,4},{24,8},{28,12},{1,17},{... | collective-permute-start | bytes 1769480 | tf_op jit(solution)/shard_map/ppermute | solution.py:631
  52.3 42.7 %collective-permute-start.1 = (bf16[512,1024]{1,0:T(8,128)(2,1)S(1)}, bf16[512,1024]{1,0:T(8,128)(2,1)}, u32[]{:S(2)}, u32[]{:S(2)}) collective-permute-start(bf16[512,1024]{1,0:T(8,128)(2,1)S(1)} %copy-done.8), channel_id=1, source_target_pairs={{1,0},{2,1},{3,2},{5,4},{6,5},{7,6},{9,8},{10,9},{11,10},{13,12},{... | collective-permute-start | bytes 3145736 | tf_op jit(solution)/shard_map/ppermute | solution.py:628
  53.8 41.3 %copy-start.7 = (s32[512]{0:T(512)}, s32[512]{0:T(512)S(1)}, u32[]{:S(2)}) copy-start(s32[512]{0:T(512)S(1)} %slice.156) | copy-start | bytes 6148
  69.8 25.3 %copy-start.9 = (bf16[3,3,128,256]{3,2,1,0:T(8,128)(2,1)}, bf16[3,3,128,256]{3,2,1,0:T(8,128)(2,1)S(1)}, u32[]{:S(2)}) copy-start(bf16[3,3,128,256]{3,2,1,0:T(8,128)(2,1)S(1)} %collective-permute-done.2.refs_16_.refs_10_) | copy-start | bytes 1769476
  69.8 25.2 %collective-permute-start.3 = (bf16[3,3,128,256]{3,2,1,0:T(8,128)(2,1)S(1)}, bf16[3,3,128,256]{3,2,1,0:T(8,128)(2,1)S(1)}, u32[]{:S(2)}, u32[]{:S(2)}) collective-permute-start(bf16[3,3,128,256]{3,2,1,0:T(8,128)(2,1)S(1)} %pad_maximum_fusion.refs_10_.refs_4_), channel_id=1, source_target_pairs={{0,4},{4,0},{8,12},{12,8},{16,20},{20,16},{24,28},{28,24},{1,5},{5... | collective-permute-start | bytes 1769480 | tf_op jit(solution)/shard_map/ppermute | solution.py:631
  84.4 10.7 %collective-permute-start.8 = (bf16[3,3,128,256]{3,2,1,0:T(8,128)(2,1)S(1)}, bf16[3,3,128,256]{3,2,1,0:T(8,128)(2,1)S(1)}, u32[]{:S(2)}, u32[]{:S(2)}) collective-permute-start(bf16[3,3,128,256]{3,2,1,0:T(8,128)(2,1)S(1)} %collective-permute-done.2.refs_16_.refs_10_), channel_id=1, source_target_pairs={{0,4},{4,0},{8,12},{12,8},{16,20},{20,16},{24,28},{28,24},{1,5},{5... | collective-permute-start | bytes 1769480 | tf_op jit(solution)/shard_map/ppermute | solution.py:631
  84.4 10.6 %collective-permute-start.5 = (bf16[3,3,128,256]{3,2,1,0:T(8,128)(2,1)}, bf16[3,3,128,256]{3,2,1,0:T(8,128)(2,1)S(1)}, u32[]{:S(2)}, u32[]{:S(2)}) collective-permute-start(bf16[3,3,128,256]{3,2,1,0:T(8,128)(2,1)} %collective-permute-done.4.refs_12_.refs_6_), channel_id=1, source_target_pairs={{0,4},{4,0},{8,12},{12,8},{16,20},{20,16},{24,28},{28,24},{1,5},{5... | collective-permute-start | bytes 1769480 | tf_op jit(solution)/shard_map/ppermute | solution.py:631
  84.9 10.1 %collective-permute-start.7 = (bf16[3,3,128,256]{3,2,1,0:T(8,128)(2,1)}, bf16[3,3,128,256]{3,2,1,0:T(8,128)(2,1)S(1)}, u32[]{:S(2)}, u32[]{:S(2)}) collective-permute-start(bf16[3,3,128,256]{3,2,1,0:T(8,128)(2,1)} %collective-permute-done.6.refs_14_.refs_8_), channel_id=1, source_target_pairs={{0,4},{4,0},{8,12},{12,8},{16,20},{20,16},{24,28},{28,24},{1,5},{5... | collective-permute-start | bytes 1769480 | tf_op jit(solution)/shard_map/ppermute | solution.py:631
  95.0 0.8 copy-start.10
  95.0 1.0 copy-start.12
  95.0 1.2 copy-start.13
  95.1 1.4 copy-start.11
  135.8 5.9 %collective-permute-start.9 = (bf16[4,4,3,128,256]{4,3,2,1,0:T(8,128)(2,1)}, bf16[4,4,3,128,256]{4,3,2,1,0:T(8,128)(2,1)S(1)}, u32[]{:S(2)}, u32[]{:S(2)}) collective-permute-start(bf16[4,4,3,128,256]{4,3,2,1,0:T(8,128)(2,1)} %get-tuple-element.72), channel_id=1, source_target_pairs={{0,4},{4,0},{8,12},{12,8},{16,20},{20,16},{24,28},{28,24},{1,5},{5... | collective-permute-start | bytes 9437192 | tf_op jit(solution)/shard_map/ppermute | solution.py:631
  144.7 31.5 %collective-permute-start.12 = (bf16[4,3,128,256]{3,2,1,0:T(8,128)(2,1)S(1)}, bf16[4,3,128,256]{3,2,1,0:T(8,128)(2,1)S(1)}, u32[]{:S(2)}, u32[]{:S(2)}) collective-permute-start(bf16[4,3,128,256]{3,2,1,0:T(8,128)(2,1)S(1)} %get-tuple-element.83), channel_id=1, source_target_pairs={{0,8},{4,12},{8,0},{12,4},{16,24},{20,28},{24,16},{28,20},{1,9},{5... | collective-permute-start | bytes 2359304 | tf_op jit(solution)/shard_map/ppermute | solution.py:631
  147.2 35.3 %collective-permute-start.13 = (bf16[4,3,128,256]{3,2,1,0:T(8,128)(2,1)S(1)}, bf16[4,3,128,256]{3,2,1,0:T(8,128)(2,1)S(1)}, u32[]{:S(2)}, u32[]{:S(2)}) collective-permute-start(bf16[4,3,128,256]{3,2,1,0:T(8,128)(2,1)S(1)} %get-tuple-element.84), channel_id=1, source_target_pairs={{0,16},{4,20},{8,24},{12,28},{16,0},{20,4},{24,8},{28,12},{1,17},{... | collective-permute-start | bytes 2359304 | tf_op jit(solution)/shard_map/ppermute | solution.py:631
  148.5 35.8 %collective-permute-start.14 = (bf16[4,3,128,256]{3,2,1,0:T(8,128)(2,1)S(1)}, bf16[4,3,128,256]{3,2,1,0:T(8,128)(2,1)S(1)}, u32[]{:S(2)}, u32[]{:S(2)}) collective-permute-start(bf16[4,3,128,256]{3,2,1,0:T(8,128)(2,1)S(1)} %get-tuple-element.85), channel_id=1, source_target_pairs={{0,24},{4,28},{8,16},{12,20},{16,8},{20,12},{24,0},{28,4},{1,25},{... | collective-permute-start | bytes 2359304 | tf_op jit(solution)/shard_map/ppermute | solution.py:631
  176.2 15.3 %copy-start.2 = (bf16[4,4,3,128,256]{4,3,2,1,0:T(8,128)(2,1)S(1)}, bf16[4,4,3,128,256]{4,3,2,1,0:T(8,128)(2,1)}, u32[]{:S(2)}) copy-start(bf16[4,4,3,128,256]{4,3,2,1,0:T(8,128)(2,1)} %get-tuple-element.80) | copy-start | bytes 9437188
  185.6 5.9 %collective-permute-start.15 = (bf16[4,4,3,128,256]{4,3,2,1,0:T(8,128)(2,1)}, bf16[4,4,3,128,256]{4,3,2,1,0:T(8,128)(2,1)S(1)}, u32[]{:S(2)}, u32[]{:S(2)}) collective-permute-start(bf16[4,4,3,128,256]{4,3,2,1,0:T(8,128)(2,1)} %get-tuple-element.86), channel_id=1, source_target_pairs={{0,4},{4,0},{8,12},{12,8},{16,20},{20,16},{24,28},{28,24},{1,5},{5... | collective-permute-start | bytes 9437192 | tf_op jit(solution)/shard_map/ppermute | solution.py:631
  192.9 20.6 %collective-permute-start.16 = (bf16[4,3,128,256]{3,2,1,0:T(8,128)(2,1)S(1)}, bf16[4,3,128,256]{3,2,1,0:T(8,128)(2,1)}, u32[]{:S(2)}, u32[]{:S(2)}) collective-permute-start(bf16[4,3,128,256]{3,2,1,0:T(8,128)(2,1)S(1)} %get-tuple-element.95), channel_id=1, source_target_pairs={{0,8},{4,12},{8,0},{12,4},{16,24},{20,28},{24,16},{28,20},{1,9},{5... | collective-permute-start | bytes 2359304 | tf_op jit(solution)/shard_map/ppermute | solution.py:631
  193.5 36.3 %collective-permute-start.17 = (bf16[4,3,128,256]{3,2,1,0:T(8,128)(2,1)S(1)}, bf16[4,3,128,256]{3,2,1,0:T(8,128)(2,1)}, u32[]{:S(2)}, u32[]{:S(2)}) collective-permute-start(bf16[4,3,128,256]{3,2,1,0:T(8,128)(2,1)S(1)} %get-tuple-element.96), channel_id=1, source_target_pairs={{0,16},{4,20},{8,24},{12,28},{16,0},{20,4},{24,8},{28,12},{1,17},{... | collective-permute-start | bytes 2359304 | tf_op jit(solution)/shard_map/ppermute | solution.py:631
  195.3 34.5 %collective-permute-start.18 = (bf16[4,3,128,256]{3,2,1,0:T(8,128)(2,1)S(1)}, bf16[4,3,128,256]{3,2,1,0:T(8,128)(2,1)}, u32[]{:S(2)}, u32[]{:S(2)}) collective-permute-start(bf16[4,3,128,256]{3,2,1,0:T(8,128)(2,1)S(1)} %get-tuple-element.97), channel_id=1, source_target_pairs={{0,24},{4,28},{8,16},{12,20},{16,8},{20,12},{24,0},{28,4},{1,25},{... | collective-permute-start | bytes 2359304 | tf_op jit(solution)/shard_map/ppermute | solution.py:631
  196.4 42.0 %collective-permute-start.10 = (bf16[512,1024]{1,0:T(8,128)(2,1)}, bf16[512,1024]{1,0:T(8,128)(2,1)}, u32[]{:S(2)}, u32[]{:S(2)}) collective-permute-start(bf16[512,1024]{1,0:T(8,128)(2,1)} %get-tuple-element.77), channel_id=1, source_target_pairs={{0,1},{1,2},{2,3},{4,5},{5,6},{6,7},{8,9},{9,10},{10,11},{12,13},{... | collective-permute-start | bytes 3145736 | tf_op jit(solution)/shard_map/ppermute | solution.py:628
  202.1 39.9 %collective-permute-start.11 = (bf16[512,1024]{1,0:T(8,128)(2,1)}, bf16[512,1024]{1,0:T(8,128)(2,1)}, u32[]{:S(2)}, u32[]{:S(2)}) collective-permute-start(bf16[512,1024]{1,0:T(8,128)(2,1)} %get-tuple-element.78), channel_id=1, source_target_pairs={{1,0},{2,1},{3,2},{5,4},{6,5},{7,6},{9,8},{10,9},{11,10},{13,12},{... | collective-permute-start | bytes 3145736 | tf_op jit(solution)/shard_map/ppermute | solution.py:628
  232.7 25.2 %all-to-all-start.1 = ((bf16[4,3,128,256]{3,2,1,0:T(8,128)(2,1)}), bf16[4,3,128,256]{3,2,1,0:T(8,128)(2,1)S(1)}, u32[]{:S(2)}, u32[]{:S(2)}) async-start(bf16[4,3,128,256]{3,2,1,0:T(8,128)(2,1)} %add_convert_fusion), calls=%async_computation.2 | async-start | bytes 1572864 | tf_op jit(solution)/shard_map/all_to_all | solution.py:682
  242.0 7.0 %copy-start.5 = (f32[8,1024]{1,0:T(8,128)S(1)}, f32[8,1024]{1,0:T(8,128)}, u32[]{:S(2)}) copy-start(f32[8,1024]{1,0:T(8,128)} %get-tuple-element.93) | copy-start | bytes 98308
  258.1 29.5 %copy-start.4 = (bf16[3,128,256]{2,1,0:T(8,128)(2,1)}, bf16[3,128,256]{2,1,0:T(8,128)(2,1)S(1)}, u32[]{:S(2)}) copy-start(bf16[3,128,256]{2,1,0:T(8,128)(2,1)S(1)} %reduce_sum.54.refs_0_) | copy-start | bytes 589828
  269.6 10.0 %all-to-all-start.3 = ((f32[32,1,288]{2,1,0:T(1,128)}), f32[32,1,288]{2,1,0:T(1,128)S(1)}, u32[]{:S(2)}, u32[]{:S(2)}) async-start(f32[32,1,288]{2,1,0:T(1,128)} %broadcast_in_dim.33), calls=%async_computation.4 | async-start | bytes 98304 | tf_op jit(solution)/shard_map/all_to_all | solution.py:802
  272.2 29.7 %all-gather.4.cloned.1.call-start = ((), (), s32[]{:S(2)}) async-start(), calls=%async_computation.6 | async-start | bytes 1769472 | tf_op jit(solution)/shard_map/all_gather | solution.py:793
  272.9 8.1 %collective-permute-start.20 = (bf16[3,128,256]{2,1,0:T(8,128)(2,1)S(1)}, bf16[3,128,256]{2,1,0:T(8,128)(2,1)S(1)}, u32[]{:S(2)}, u32[]{:S(2)}) collective-permute-start(bf16[3,128,256]{2,1,0:T(8,128)(2,1)S(1)} %reduce_sum.54.refs_0_), channel_id=1, source_target_pairs={{0,8},{4,12},{8,0},{12,4},{16,24},{20,28},{24,16},{28,20},{1,9},{5... | collective-permute-start | bytes 589832 | tf_op jit(solution)/shard_map/ppermute | solution.py:631
  274.6 11.2 %collective-permute-start.22 = (bf16[3,128,256]{2,1,0:T(8,128)(2,1)S(1)}, bf16[3,128,256]{2,1,0:T(8,128)(2,1)S(1)}, u32[]{:S(2)}, u32[]{:S(2)}) collective-permute-start(bf16[3,128,256]{2,1,0:T(8,128)(2,1)S(1)} %reduce_sum.54.refs_0_), channel_id=1, source_target_pairs={{0,16},{4,20},{8,24},{12,28},{16,0},{20,4},{24,8},{28,12},{1,17},{... | collective-permute-start | bytes 589832 | tf_op jit(solution)/shard_map/ppermute | solution.py:631
  276.1 9.7 %collective-permute-start.24 = (bf16[3,128,256]{2,1,0:T(8,128)(2,1)S(1)}, bf16[3,128,256]{2,1,0:T(8,128)(2,1)S(1)}, u32[]{:S(2)}, u32[]{:S(2)}) collective-permute-start(bf16[3,128,256]{2,1,0:T(8,128)(2,1)S(1)} %reduce_sum.54.refs_0_), channel_id=1, source_target_pairs={{0,24},{4,28},{8,16},{12,20},{16,8},{20,12},{24,0},{28,4},{1,25},{... | collective-permute-start | bytes 589832 | tf_op jit(solution)/shard_map/ppermute | solution.py:631
  276.5 10.9 %collective-permute-start.19 = (bf16[3,128,256]{2,1,0:T(8,128)(2,1)S(1)}, bf16[3,128,256]{2,1,0:T(8,128)(2,1)S(1)}, u32[]{:S(2)}, u32[]{:S(2)}) collective-permute-start(bf16[3,128,256]{2,1,0:T(8,128)(2,1)S(1)} %reduce_sum.54.refs_0_), channel_id=1, source_target_pairs={{0,4},{4,0},{8,12},{12,8},{16,20},{20,16},{24,28},{28,24},{1,5},{5... | collective-permute-start | bytes 589832 | tf_op jit(solution)/shard_map/ppermute | solution.py:631
  281.0 6.5 %copy-start.14 = (bf16[3,128,256]{2,1,0:T(8,128)(2,1)}, bf16[3,128,256]{2,1,0:T(8,128)(2,1)S(1)}, u32[]{:S(2)}) copy-start(bf16[3,128,256]{2,1,0:T(8,128)(2,1)S(1)} %collective-permute-done.20.refs_2_) | copy-start | bytes 589828
  281.0 6.4 %collective-permute-start.21 = (bf16[3,128,256]{2,1,0:T(8,128)(2,1)S(1)}, bf16[3,128,256]{2,1,0:T(8,128)(2,1)S(1)}, u32[]{:S(2)}, u32[]{:S(2)}) collective-permute-start(bf16[3,128,256]{2,1,0:T(8,128)(2,1)S(1)} %collective-permute-done.20.refs_2_), channel_id=1, source_target_pairs={{0,4},{4,0},{8,12},{12,8},{16,20},{20,16},{24,28},{28,24},{1,5},{5... | collective-permute-start | bytes 589832 | tf_op jit(solution)/shard_map/ppermute | solution.py:631
  285.8 1.7 copy-start.15
  285.8 1.7 collective-permute-start.23
  285.8 1.7 copy-start.16
  285.8 1.7 collective-permute-start.25
  287.4 0.7 copy-start.17
  287.5 0.7 copy-start.18
  287.5 0.8 copy-start.19
  288.3 0.7 copy-start.20
  301.9 3.6 %copy-start.1 = (bf16[1024,256]{1,0:T(8,128)(2,1)S(1)}, bf16[1024,256]{1,0:T(8,128)(2,1)}, u32[]{:S(2)}) copy-start(bf16[1024,256]{1,0:T(8,128)(2,1)} %param.33) | copy-start | bytes 1572868
Sparse Core Ops, SparseCore 0:
  11.5 90.9 all-gather.5
  204.3 33.4 reduce-scatter.1
  274.9 26.9 all-gather.3
where the time goes:
time: 317 us; the launch traced here: 312 us
  waiting for transfers between devices  140 us (44%)
  Pallas kernels  78.7 us (25%)
  starting transfers between devices  42.2 us (13%)
  between operations  15.2 us (5%)
  local copies, waits for them, and re-layouts  13.6 us (4%)
  other arithmetic  12.1 us (4%)
  blocking collectives  10.7 us (3%)
    ppermute x22, waiting for transfers between devices, swap(): return lax.ppermute(x, 'seq', [(i, i ^ mask) for i in range(n_seq)])  80.4 us
    pallas_call x6, Pallas kernels, call(): pl.pallas_call(kernel, out_shape=tuple((jax.ShapeDtypeStruct(*o) for o in...  78.7 us
    all_to_all x1, waiting for transfers between devices, over_tp(): got = lax.all_to_all(block, 'tp', 0, 0, tiled=True)  26.4 us
    ppermute x22, starting transfers between devices, swap(): return lax.ppermute(x, 'seq', [(i, i ^ mask) for i in range(n_seq)])  17 us
    all_to_all x1, blocking collectives, body(): vectors = lax.all_to_all(vectors, ('seq', 'tp'), 0, 0, tiled=True)  10.7 us
    ppermute x4, waiting for transfers between devices, shift(): return lax.ppermute(x, 'tp', pairs)  10.7 us
    ppermute x4, starting transfers between devices, shift(): return lax.ppermute(x, 'tp', pairs)  10.5 us
    all_gather x1, waiting for transfers between devices, body(): feed_g = lax.all_gather(feed_g.reshape(piece), 'seq', axis=0)[:inner]  9.63 us
  transfers between devices with their start and end apart: 32, of which 15 were waited for; matrix products, arithmetic and copies ran while one was open for 5% of the time, Pallas kernels for 17%

commit v1 on v0

--- a/solution.py
+++ b/solution.py
@@ -69,12 +69,6 @@
     s, t = meta[0], meta[1]
     count, size, per = pieces[0].shape[1:]
     n_tp = dst.shape[2] // per
-    if len(pieces) == 1:
-        for i in range(pieces[0].shape[0]):
-            at, to = i // n_tp * size, i % n_tp * per
-            target = dst.at[:, at : at + size, to : to + per]
-            pltpu.make_async_copy(pieces[0].at[i], target, sem).start()
-        return pltpu.make_async_copy(dst, dst, sem).wait
     mine = pl.ds(pl.multiple_of(t * per, per), per)
     for m in range(count):
         source = shards[m].at[:, off : off + per]
@@ -89,21 +83,27 @@
 
 def store_grads(meta, grads, keep, send, sems, first, last):
     s = meta[0]
-    half, n_tp, _, size, per = keep.shape
+    n_tp, _, size, per = keep[0].shape
     for parity, dst in enumerate((keep, send)):
-        for jj in range(half):
+        for jj, piece in enumerate(dst):
             p = pl.ds(pl.multiple_of((s ^ (2 * jj + parity)) * size, size), size)
             for t in range(n_tp):
                 pltpu.make_async_copy(
                     grads.at[first:last, p, t * per : (t + 1) * per],
-                    dst.at[jj, t, first:last],
-                    sems.at[parity],
+                    piece.at[t, first:last],
+                    sems.at[parity, jj],
                 ).start()
 
 
 def grads_stored(keep, send, sems):
     for parity, dst in enumerate((keep, send)):
-        pltpu.make_async_copy(dst, dst, sems.at[parity]).wait()
+        for jj, piece in enumerate(dst):
+            pltpu.make_async_copy(piece, piece, sems.at[parity, jj]).wait()
+
+
+def travelling(inner, width, per):
+    half = max(inner // 2, 1)
+    return half, (width // SHARD, 3, width // inner, per)
 
 
 def attend(rng, segq, segk, q, k, v, mixed, lse, s_scr, m_scr, l_scr, acc):
@@ -309,15 +309,16 @@
     )
 
 
-def feed_kernel(n_pieces, groups, meta, inputs, dout, bo, gain, shift, bup, bdn, *refs):
+def feed_kernel(n_pieces, half, groups, meta, inputs, dout, bo, gain, shift, bup, bdn, *refs):
     parts, refs = refs[:groups], refs[groups:]
-    pieces, refs = refs[:n_pieces], refs[n_pieces:]
+    shards, pieces, refs = refs[:3], refs[3 : 3 + n_pieces], refs[3 + n_pieces :]
     g_parts, refs = refs[:groups], refs[groups:]
     deltas, refs = refs[:groups], refs[groups:]
-    sums, output_out, g_resid_out, keep, send, *refs = refs
+    sums, output_out, g_resid_out, *refs = refs
+    keep, send, refs = refs[:half], refs[half : 2 * half], refs[2 * half :]
     w, mixed, resid, hat, rstd, second, hidden, g_up, g_sec, low, output, grads, *sems = refs
     sem, grad_sems, out_sems = sems
-    wait = load_weights(meta, None, 0, pieces, w, sem)
+    wait = load_weights(meta, shards, 0, pieces, w, sem)
     wo_t, wup, wdn_t = w.at[0], w.at[1], w.at[2]
     tokens, width = inputs.shape
     per = SHARD // groups
@@ -391,19 +392,22 @@
     grads_stored(keep, send, grad_sems)
 
 
-def feed_forward(meta, inner, inputs, dout, bo, gain, shift, bup, bdn, parts, pieces):
+def feed_forward(
+    meta, inner, inputs, dout, bo, gain, shift, bup, bdn, parts, shards, pieces
+):
     tokens, width = inputs.shape
     groups = len(parts)
-    half = max(inner // 2, 1)
-    travel = ((half, width // SHARD, 3, width // inner, SHARD), BF16)
+    half, piece = travelling(inner, width, SHARD)
+    travel = [(piece, BF16)] * (2 * half)
     wide = pltpu.VMEM((tokens, width), F32)
     slim = pltpu.VMEM((tokens, width), BF16)
     return call(
-        functools.partial(feed_kernel, len(pieces), groups),
+        functools.partial(feed_kernel, len(pieces), half, groups),
         [(parts[0].shape, BF16)] * groups
         + [((width // HEAD_DIM // groups, tokens), F32)] * groups
-        + [((8, width), F32), ((tokens, width), BF16), ((tokens, width), F32), travel, travel],
-        [meta, inputs, dout, bo, gain, shift, bup, bdn, *parts, *pieces],
+        + [((8, width), F32), ((tokens, width), BF16), ((tokens, width), F32)]
+        + travel,
+        [meta, inputs, dout, bo, gain, shift, bup, bdn, *parts, *shards, *pieces],
         [
             pltpu.VMEM((3, width, width), BF16),
             slim,
@@ -418,26 +422,22 @@
             slim,
             pltpu.VMEM((3, width, width), BF16),
             pltpu.SemaphoreType.DMA,
-            pltpu.SemaphoreType.DMA((2,)),
+            pltpu.SemaphoreType.DMA((2, half)),
             pltpu.SemaphoreType.DMA((2,)),
         ],
         "feed_forward",
         smem=1,
-        anys=len(pieces),
-        out_anys=4,
+        anys=3 + len(pieces),
+        out_anys=2 + 2 * half,
     )
 
 
-def backward_kernel(n_pieces, off, more, meta, rng, segq, segk, lse, delta, q, do, k, v, *refs):
-    if more:
-        left_in, right_in, *refs = refs
-    low_in, *refs = refs
-    shards, pieces, refs = refs[:3], refs[3 : 3 + n_pieces], refs[3 + n_pieces :]
-    left, own, right, sums, keep, send, *refs = refs
-    low, w, dq, dk, dv, dk_acc, dv_acc, dq_acc, grads, sem, low_sem, grad_sems = refs
-    low_copy = pltpu.make_async_copy(low_in, low, low_sem)
+def backward_kernel(half, meta, rng, segq, segk, lse, delta, q, do, k, v, low_in, *refs):
+    sums, dq_out, dk_out, dv_out, keep, send, *refs = refs
+    keep, send = [[x.at[jj] for jj in range(half)] for x in (keep, send)]
+    low, dq, dk, dv, dk_acc, dv_acc, dq_acc, grads, sems, grad_sems = refs
+    low_copy = pltpu.make_async_copy(low_in, low, sems.at[3])
     low_copy.start()
-    wait = load_weights(meta, shards, off, pieces, w, sem)
     tokens, width = q.shape
     start, stop = tokens - FAR, 2 * tokens + FAR
     near, middle = slice(start, stop), slice(tokens, 2 * tokens)
@@ -461,16 +461,20 @@
     attend_back(rng, segq, segk, lse, delta, q, do, k, v, dq, dk_acc, dv_acc, dq_acc)
     narrow(near)
     ends(narrow)
+    outs = [
+        pltpu.make_async_copy(x, out, sems.at[i])
+        for i, (x, out) in enumerate(((dq, dq_out), (dk, dk_out), (dv, dv_out)))
+    ]
+    for x in outs:
+        x.start()
 
     low_copy.wait()
     grads[0] = dot_tn(low[middle, :], dq[...]).astype(BF16)
+    grads[1] = dot_tn(low[near, :], dk[near, :]).astype(BF16)
+    grads[2] = dot_tn(low[near, :], dv[near, :]).astype(BF16)
     sums[...] = jnp.zeros(sums.shape, F32)
     sums[0:1, :] = jnp.sum(dq[...].astype(F32), axis=0, keepdims=True)
-
     sums[1:2, :] = jnp.sum(dv[near, :].astype(F32), axis=0, keepdims=True)
-    grads[1] = dot_tn(low[near, :], dk[near, :]).astype(BF16)
-    grads[2] = dot_tn(low[near, :], dv[near, :]).astype(BF16)
-
     for i, used in enumerate((before, after)):
 
         @pl.when(used)
@@ -482,8 +486,59 @@
                 grads[m] = (grads[m].astype(F32) + more).astype(BF16)
 
     store_grads(meta, grads, keep, send, grad_sems, 0, 3)
-
+    for x in outs:
+        x.wait()
+    grads_stored(keep, send, grad_sems)
+
+
+def backward(meta, rng, segq, segk, lse, delta, q, do, k, v, low, inner):
+    tokens, cols = q.shape
+    width = low.shape[1]
+    window = 3 * tokens
+    per = cols // (width // SHARD)
+    half, piece = travelling(inner, width, per)
+    travel = [((half, *piece), BF16)] * 2
+    slim, wide = (tokens, cols), (window, cols)
+    return call(
+        functools.partial(backward_kernel, half),
+        [((8, cols), F32), (slim, BF16), (wide, BF16), (wide, BF16)] + travel,
+        [meta, rng, segq, segk, lse, delta, q, do, k, v, low],
+        [
+            pltpu.VMEM((window, width), BF16),
+            pltpu.VMEM(slim, BF16),
+            pltpu.VMEM(wide, BF16),
+            pltpu.VMEM(wide, BF16),
+            pltpu.VMEM(wide, F32),
+            pltpu.VMEM(wide, F32),
+            pltpu.VMEM((cols // HEAD_DIM, HEAD_DIM, BLOCK), F32),
+            pltpu.VMEM((3, width, cols), BF16),
+            pltpu.SemaphoreType.DMA((4,)),
+            pltpu.SemaphoreType.DMA((2, half)),
+        ],
+        "backward_attention",
+        smem=2,
+        anys=1,
+        out_anys=5,
+    )
+
+
+def halo_grads_kernel(n_pieces, off, more, meta, rng, *refs):
+    if more:
+        left_in, right_in, *refs = refs
+    ins, refs = refs[:2], refs[2:]
+    shards, pieces, refs = refs[:3], refs[3 : 3 + n_pieces], refs[3 + n_pieces :]
+    left, right, dk, dv, w, sem, sems = refs
+    wait = load_weights(meta, shards, off, pieces, w, sem)
+    loads = [
+        pltpu.make_async_copy(x, to, sems.at[i]) for i, (x, to) in enumerate(zip(ins, (dk, dv)))
+    ]
+    for x in loads:
+        x.start()
+    tokens = left.shape[0]
+    before, after = used_chunks(rng)
     wait()
+    for x in loads:
+        x.wait()
 
     def halo_grads(out, old, to, rows):
         res = dot_nt(dk[rows, :], w[1]) + dot_nt(dv[rows, :], w[2])
@@ -510,47 +565,90 @@
             else:
                 out[far_to, :] = jnp.zeros((tokens - FAR, out.shape[1]), BF16)
 
-    own[...] = (
-        dot_nt(dk[middle, :], w[1]) + dot_nt(dv[middle, :], w[2]) + dot_nt(dq[...], w[0])
-    )
-    grads_stored(keep, send, grad_sems)
-
-
-def backward(group, meta, rng, segq, segk, lse, delta, q, do, k, v, old, low, shards, pieces):
-    tokens, cols = q.shape
-    width = low.shape[1]
-    window = 3 * tokens
+
+def halo_grads(group, meta, rng, old, dk, dv, shards, pieces):
+    cols = dk.shape[1]
+    width = shards[0].shape[0]
     per = pieces[0].shape[3]
-    travel = ((max(len(pieces) // 2, 1), cols // per, *pieces[0].shape[1:]), BF16)
-    slim, wide, full = (tokens, cols), (window, cols), (tokens, width)
+    full = (dk.shape[0] // 3, width)
     return call(
-        functools.partial(backward_kernel, len(pieces), group * per, len(old) > 0),
-        [(full, BF16), (full, F32), (full, BF16), ((8, cols), F32), travel, travel],
-        [meta, rng, segq, segk, lse, delta, q, do, k, v, *old, low, *shards, *pieces],
+        functools.partial(halo_grads_kernel, len(pieces), group * per, len(old) > 0),
+        [(full, BF16), (full, BF16)],
+        [meta, rng, *old, dk, dv, *shards, *pieces],
         [
-            pltpu.VMEM((window, width), BF16),
+            pltpu.VMEM(dk.shape, BF16),
+            pltpu.VMEM(dv.shape, BF16),
             pltpu.VMEM((3, width, cols), BF16),
-            pltpu.VMEM(slim, BF16),
-            pltpu.VMEM(wide, BF16),
-            pltpu.VMEM(wide, BF16),
-            pltpu.VMEM(wide, F32),
-            pltpu.VMEM(wide, F32),
-            pltpu.VMEM((cols // HEAD_DIM, HEAD_DIM, BLOCK), F32),
-            pltpu.VMEM((3, width, cols), BF16),
-            pltpu.SemaphoreType.DMA,
             pltpu.SemaphoreType.DMA,
             pltpu.SemaphoreType.DMA((2,)),
         ],
-        "backward_attention",
+        "halo_grads",
         smem=2,
-        anys=4 + len(pieces),
-        out_anys=2,
+        anys=5 + len(pieces),
     )
 
 
+def input_grads_kernel(n_pieces, off, count, meta, rng, *refs):
+    ins, refs = refs[:8], refs[8:]
+    shards, pieces, refs = refs[:3], refs[3 : 3 + n_pieces], refs[3 + n_pieces :]
+    own, sums, dq, dk, dv, *refs = refs
+    x_left, x_own, x_right, left, right, w, sem, sems = refs
+    tokens = dq.shape[0]
+    wait = load_weights(meta, shards, off, pieces, w, sem)
+    middle = pl.ds(tokens, tokens)
+    ins = (ins[0], ins[1].at[middle], ins[2].at[middle], *ins[3:])
+    loads = [
+        pltpu.make_async_copy(x, to, sems.at[i])
+        for i, (x, to) in enumerate(zip(ins, (dq, dk, dv, x_left, x_own, x_right, left, right)))
+    ]
+    for x in loads:
+        x.start()
+    before, after = used_chunks(rng)
+    wait()
+    for x in loads:
+        x.wait()
+    own[...] = dot_nt(dk[...], w[1]) + dot_nt(dv[...], w[2]) + dot_nt(dq[...], w[0])
+    sums[...] = jnp.zeros(sums.shape, F32)
+
+    def tally(grad, x, lo, hi):
+        @pl.loop(lo, hi)
+        def _(i):
+            rows = pl.ds(pl.multiple_of(i * ROWS, ROWS), ROWS)
+            hat, _ = normalise(x[rows, :].astype(F32))
+            g = grad[rows, :].astype(F32)
+            sums[0:1, :] += jnp.sum(g * hat, axis=0, keepdims=True)
+            sums[1:2, :] += jnp.sum(g, axis=0, keepdims=True)
+
+    tally(own, x_own, 0, tokens // ROWS)
+    if count:
+        tally(left, x_left, jnp.where(before, 0, (tokens - FAR) // ROWS), tokens // ROWS)
+        tally(right, x_right, 0, jnp.where(after, tokens, FAR) // ROWS)
+
+
+def input_grads(group, meta, rng, dq, dk, dv, window, halos, count, shards, pieces):
+    tokens, cols = dq.shape
+    width = shards[0].shape[0]
+    per = pieces[0].shape[3]
+    full = (tokens, width)
+    return call(
+        functools.partial(input_grads_kernel, len(pieces), group * per, count),
+        [(full, F32), ((8, width), F32)],
+        [meta, rng, dq, dk, dv, *window, *halos, *shards, *pieces],
+        [pltpu.VMEM(dq.shape, BF16)] * 3
+        + [pltpu.VMEM(full, BF16)] * 5
+        + [
+            pltpu.VMEM((3, width, cols), BF16),
+            pltpu.SemaphoreType.DMA,
+            pltpu.SemaphoreType.DMA((8,)),
+        ],
+        "input_grads",
+        smem=2,
+        anys=11 + len(pieces),
+    )
+
+
 def last_kernel(inputs, g_resid, from_left, from_right, gain, *refs):
-    *owns, g_inputs, sums = refs
-    sums[...] = jnp.zeros(sums.shape, F32)
+    *owns, g_inputs = refs
 
     @pl.loop(0, inputs.shape[0] // ROWS)
     def _(i):
@@ -560,26 +658,24 @@
         for own in owns:
             g = g + own[rows, :]
         g_inputs[rows, :] = (g_resid[rows, :] + norm_back(g, hat, rstd, gain[...])).astype(BF16)
-        sums[0:1, :] += jnp.sum(g * hat, axis=0, keepdims=True)
-        sums[1:2, :] += jnp.sum(g, axis=0, keepdims=True)
 
 
 def last_step(inputs, g_resid, from_left, from_right, gain, owns):
     return call(
         last_kernel,
-        [(inputs.shape, BF16), ((8, inputs.shape[1]), F32)],
+        [(inputs.shape, BF16)],
         [inputs, g_resid, from_left, from_right, gain, *owns],
         [],
         "input_norm_grads",
     )
 
 
-def lay_out_kernel(turned, groups, meta, *refs):
+def lay_out_kernel(turned, groups, size, meta, *refs):
     outs = refs[-len(turned) :]
     pieces = refs[: -len(turned)]
     n = len(pieces) // groups
     s = meta[0]
-    size, per = pieces[0].shape[-2:]
+    per = pieces[0].shape[-1]
     for g in range(groups):
         to = slice(g * per, (g + 1) * per)
         if n == 1:
@@ -594,18 +690,19 @@
             ]
         for piece, at in whole:
             for m, turn in enumerate(turned):
+                part = piece[m, :size].astype(F32)
                 if turn:
-                    outs[m][to, at] = jnp.transpose(piece[m].astype(F32))
+                    outs[m][to, at] = jnp.transpose(part)
                 else:
-                    outs[m][at, to] = piece[m].astype(F32)
-
-
-def lay_out(meta, groups, turned):
+                    outs[m][at, to] = part
+
+
+def lay_out(meta, width, groups, turned):
     first = groups[0]
-    width = first[0].shape[-2] * (len(first) if len(first) > 1 else first[0].shape[0])
+    size = width // (len(first) if len(first) > 1 else first[0].shape[0])
     shapes = [(SHARD, width) if turn else (width, SHARD) for turn in turned]
     return call(
-        functools.partial(lay_out_kernel, turned, len(groups)),
+        functools.partial(lay_out_kernel, turned, len(groups), size),
         [(shape, F32) for shape in shapes],
         [meta, *[piece for group in groups for piece in group]],
         [],
@@ -614,6 +711,15 @@
     )
 
 
+def pause_kernel(x, out):
+    out[...] = x[...]
+
+
+def pause(x):
+    (out,) = call(pause_kernel, [(x.shape, x.dtype)], [x], [], "pause")
+    return out
+
+
 SHARD = 256
 
 
@@ -633,28 +739,32 @@
     def tie(*xs):
         return lax.optimization_barrier(xs)
 
-    def over_tp(shards, biases, off, per, s, t, after):
+    def block_of(shards, biases, off, per, s):
         size = shards[0].shape[0] // inner
         cut = jnp.stack([lax.dynamic_slice(w, (s * size, off), (size, per)) for w in shards])
-        parts = []
-        rest = jnp.stack([b[off : off + per] for b in biases])
-        for _ in range(3):
-            part = rest.astype(BF16)
-            rest = rest - part.astype(F32)
-            parts.append(part)
-        parts = jnp.stack(parts + [jnp.zeros_like(parts[0])] * 13, axis=1)
-        block = jnp.concatenate([cut, parts], axis=1)
-        block = jnp.broadcast_to(block[None], (n_tp, *block.shape))
-        if after is not None:
-            block, _ = tie(block, after)
-        got = lax.all_to_all(block, "tp", 0, 0, tiled=True)
-        others = jnp.stack(
+        if biases:
+            parts = []
+            rest = jnp.stack([b[off : off + per] for b in biases])
+            for _ in range(3):
+                part = rest.astype(BF16)
+                rest = rest - part.astype(F32)
+                parts.append(part)
+            parts = jnp.stack(parts + [jnp.zeros_like(parts[0])] * 13, axis=1)
+            cut = jnp.concatenate([cut, parts], axis=1)
+        return jnp.broadcast_to(cut[None], (n_tp, *cut.shape))
+
+    def over_tp(block):
+        return lax.all_to_all(block, "tp", 0, 0, tiled=True)
+
+    def others_of(got, size, t):
+        return jnp.stack(
             [lax.dynamic_index_in_dim(got, lax.rem(t + r + 1, n_tp), 0, keepdims=False)[:, :size]
              for r in range(n_tp - 1)]
         )
+
+    def biases_of(got, size):
         whole = jnp.sum(got[:, :, size : size + 3].astype(F32), axis=2)
-        whole = [whole[:, m].reshape(1, n_tp * per) for m in range(len(biases))]
-        return others, whole, got
+        return [whole[:, m].reshape(1, -1) for m in range(whole.shape[1])]
 
     def from_chips(x):
         return [x] + [swap(x, mask) for mask in masks]
@@ -663,14 +773,15 @@
         odd = [swap(e, 1) for e in even]
         return [e for pair in zip(even, odd) for e in pair]
 
-    def over_cores(keep, send):
-        got = swap(send, 1)
-        return [(keep[jj].astype(F32) + got[jj].astype(F32)).astype(BF16) for jj in range(half)]
+    def core_sums(keep, got):
+        return [(k.astype(F32) + g.astype(F32)).astype(BF16) for k, g in zip(keep, got)]
 
     def over_chips(sums):
-        moved = [swap(sums[jj], 2 * jj) for jj in range(1, half)]
-        total = sums[0].astype(F32)
-        for x in moved:
+        return [sums[0]] + [swap(sums[jj], 2 * jj) for jj in range(1, half)]
+
+    def chip_sum(moved):
+        total = moved[0].astype(F32)
+        for x in moved[1:]:
             total = total + x.astype(F32)
         total = total.astype(BF16)
         if outer > 1:
@@ -705,21 +816,20 @@
 
         attn_w = [w_query, w_key, w_value]
         attn_b = [b_query, b_up, b_value]
-        done, dones = None, []
+        size = width // inner
+        feed_w = [w_out.T, w_up, w_down.T]
+        feed_block = block_of(feed_w, [], 0, SHARD, s)
         attn_p, attn_whole = [], []
         for g in every:
-            others, whole, done = over_tp(attn_w, attn_b, g * per, per, s, t, done)
-            dones.append(done)
-            even = from_chips(others)
-            even[0], _ = tie(even[0], even[-1])
+            got = over_tp(block_of(attn_w, attn_b, g * per, per, s))
+            got, feed_block = tie(got, feed_block)
+            even = from_chips(others_of(got, size, t))
+            even[0], even[-1] = tie(even[0], even[-1])
             attn_p.append(from_cores(even))
-            attn_whole.append(whole)
-        feed_w = [w_out.T, w_up, w_down.T]
-        size = width // n_seq
-        at = lax.axis_index("seq") * size
-        cut = jnp.stack([lax.dynamic_slice_in_dim(w, at, size, 0) for w in feed_w])
-        feed_p = [lax.all_gather(cut, ("seq", "tp"), axis=0)]
-        inputs_later, _ = tie(inputs, dones[0])
+            attn_whole.append(biases_of(got, size))
+        got = over_tp(feed_block)
+        inputs_later, got = tie(inputs, got)
+        feed_p = from_chips(others_of(got, size, t))
         left = shift(inputs_later, 1)
         right = shift(inputs_later, -1)
 
@@ -737,7 +847,8 @@
         rng = jnp.stack([low // BLOCK, (high + BLOCK - 1) // BLOCK])
         segq, segk = seg_mine[None, :], seg_win[:, None]
 
-        source = (row(norm1_gain), row(norm1_shift), left, inputs, right)
+        gain1, feed_w[0], feed_w[2] = tie(norm1_gain, feed_w[0], feed_w[2])
+        source = (row(gain1), row(norm1_shift), left, inputs, right)
         saved = []
         for g in every:
             bq, _, bv = attn_whole[g]
@@ -745,67 +856,80 @@
             mixed, lse, q, k, v = res[:5]
             if g == 0:
                 source = first_low = res[5]
+                mixed, *feed_p = tie(mixed, *feed_p)
+                feed_p = from_cores(feed_p)
             saved.append((mixed, lse, q, k, v))
         bup = by_shard([x[1] for x in attn_whole])
         res = feed_forward(
             meta, inner, inputs, out_grad, row(b_out), row(norm2_gain), row(norm2_shift), bup,
-            row(b_down), [x[0] for x in saved], feed_p,
+            row(b_down), [x[0] for x in saved], feed_w, feed_p,
         )
         g_mixed, delta = list(res[:GROUPS]), res[GROUPS : 2 * GROUPS]
-        sums_feed, output, g_resid, keep, send = res[2 * GROUPS :]
-
-        sums = over_cores(keep, send)
-        g_mixed[0], *sums = tie(g_mixed[0], *sums)
-        feed_total = over_chips(sums)
+        sums_feed, output, g_resid, *travel = res[2 * GROUPS :]
+
+        sums = core_sums(travel[:half], [swap(x, 1) for x in travel[half:]])
+        feed_moved = over_chips(sums)
+        g_mixed[0], *feed_moved[:1] = tie(g_mixed[0], *feed_moved[:1])
         old, owns, sums_qkv, totals = (), [], [], []
         for g in every:
             _, lse, q, k, v = saved[g]
-            dx_left, own, dx_right, vec, keep, send = backward(
-                g, meta, rng, segq, segk, lse, delta[g], q, g_mixed[g], k, v, old,
-                first_low, attn_w, attn_p[g],
+            vec, dq, dk, dv, keep, send = backward(
+                meta, rng, segq, segk, lse, delta[g], q, g_mixed[g], k, v, first_low, inner
             )
-            old = (dx_left, dx_right)
+            sums_qkv.append(vec)
+            got = swap(send, 1)
+            if g == 0:
+                feed_total = chip_sum(feed_moved)
+                feed_total, sums_feed = tie(feed_total, sums_feed)
+                got, sums_feed = tie(got, pause(sums_feed))
+            sums = [None] * half
+            for jj in reversed(range(half)):
+                (sums[jj],) = core_sums(keep[jj : jj + 1], got[jj : jj + 1])
+                keep, got, sums[jj] = tie(keep, got, sums[jj])
+            if g + 1 == GROUPS:
+                dk, *sums = tie(dk, *sums)
+            old = halo_grads(g, meta, rng, old, dk, dv, attn_w, attn_p[g])
+            own, sums_in = input_grads(
+                g, meta, rng, dq, dk, dv, (left, inputs, right), old, g + 1 == GROUPS,
+                attn_w, attn_p[g],
+            )
+            if g + 1 < GROUPS:
+                g_mixed[g + 1], own, *sums = tie(g_mixed[g + 1], own, *sums)
             owns.append(own)
-            sums_qkv.append(vec)
-            if g > 0:
-                send, totals[g - 1] = tie(send, totals[g - 1])
-            else:
-                send, feed_total = tie(send, feed_total)
-            sums = over_cores(keep, send)
-            if g + 1 < GROUPS:
-                g_mixed[g + 1], *sums = tie(g_mixed[g + 1], *sums)
-            else:
-                owns[g], *sums = tie(owns[g], *sums)
-            totals.append(over_chips(sums))
-        from_right = shift(dx_left, -1)
-        from_left = shift(dx_right, 1)
+            moved = over_chips(sums)
+            if g + 1 == GROUPS:
+                feed_g = feed_total.reshape(-1, SHARD)
+                feed_g = lax.psum_scatter(feed_g, "tp", scatter_dimension=0, tiled=True)
+                moved[0], sums_in, feed_g = tie(moved[0], sums_in, feed_g)
+            totals.append(chip_sum(moved))
+        from_right = shift(old[0], -1)
+        from_left = shift(old[1], 1)
         piece = feed_total.shape[1:]
-        feed_g = feed_total.reshape(-1, SHARD)
-        feed_g = lax.psum_scatter(feed_g, "tp", scatter_dimension=0, tiled=True)
-        shards = []
-        for g in every:
-            shards.append(own_shard(totals[g]))
-        g_inputs, sums_in = last_step(
+        feed_g = lax.all_gather(feed_g.reshape(piece), "seq", axis=0)[:inner]
+        (g_inputs,) = last_step(
             inputs, g_resid, from_left, from_right, row(norm1_gain), owns
         )
 
-        g_inputs, feed_g = tie(g_inputs, feed_g)
-        feed_g = lax.all_gather(feed_g.reshape(piece), "seq", axis=0)[:inner]
         vectors = [by_shard([x[i] for x in sums_qkv]) for i in range(2)]
-        vectors = [sums_in[:2], *vectors, sums_feed[:5]]
-        vectors = jnp.concatenate(vectors)
-        n_vec = vectors.shape[0]
-        vectors, shards[-1] = tie(vectors, shards[-1])
-        vectors = vectors.reshape(n_seq * n_tp, -1)
-        vectors = lax.all_to_all(vectors, ("seq", "tp"), 0, 0, tiled=True)
-        vectors = jnp.broadcast_to(jnp.sum(vectors, axis=0, keepdims=True), vectors.shape)
-        vectors = lax.all_to_all(vectors, ("seq", "tp"), 0, 0, tiled=True)
-        vectors = vectors.reshape(n_vec, width)
+        vectors = jnp.concatenate([sums_in[:2], *vectors, sums_feed[:5]])
+        if outer > 1:
+            groups = [[i + inner * o for o in range(outer)] for i in range(inner)]
+            vectors = lax.psum(vectors, "seq", axis_index_groups=groups)
+        extra = -(-vectors.size // (48 * per)) * 16
+        n_vec = vectors.size
+        vectors = jnp.pad(vectors.astype(BF16).reshape(-1), (0, 3 * extra * per - n_vec))
+        vectors = jnp.broadcast_to(vectors.reshape(1, 3, extra, per), (n_tp, 3, extra, per))
+        totals[-1] = jnp.concatenate([totals[-1], vectors], axis=2)
+        shards = [own_shard(x) for x in totals]
+        shards[-1], g_inputs = tie(shards[-1], g_inputs)
+        pieces = [from_cores(from_chips(x)) for x in shards]
+        vectors = sum([x[:, size:].astype(F32) for x in pieces[-1]])
+        vectors = vectors.reshape(-1)[:n_vec].reshape(-1, width)
         n1g, n1s, g_bq, g_bv, g_bo, n2g, n2s, g_bup, g_bdn = [vectors[i] for i in range(9)]
 
-        pieces = [from_cores(from_chips(x)) for x in shards]
-        g_wq, g_wk, g_wv = lay_out(meta, pieces, (False, False, False))
-        g_wo, g_wup, g_wdn = lay_out(meta, [[feed_g]], (True, False, True))
+        g_wo, g_wup, g_wdn = lay_out(meta, width, [[feed_g]], (True, False, True))
+        g_wup, pieces[-1][1] = tie(g_wup, pieces[-1][1])
+        g_wq, g_wk, g_wv = lay_out(meta, width, pieces, (False, False, False))
 
         def shard(x):
             return lax.dynamic_slice_in_dim(x, t * SHARD, SHARD, 0)

time: 317 us -> 297 us (0.937)
  waiting for transfers between devices: 140 us -> 85.7 us
  Pallas kernels: 78.7 us -> 102 us
  starting transfers between devices: 42.2 us -> 58.1 us
  blocking collectives: 10.7 us -> 0 us
  other arithmetic: 12.1 us -> 16.3 us
    ppermute x22 -> x32, waiting for transfers between devices: 80.4 us -> 36.2 us  [swap(): return lax.ppermute(x, 'seq', [(i, i ^ mask) for i in range(n_seq)])]
    pallas_call x6 -> x9, Pallas kernels: 78.7 us -> 102 us  [call(): pl.pallas_call(kernel, out_shape=tuple((jax.ShapeDtypeStruct(*o) for o in...]
    all_to_all x1 -> x0, blocking collectives: 10.7 us -> none  [body(): vectors = lax.all_to_all(vectors, ('seq', 'tp'), 0, 0, tiled=True)]
    all_gather x1, waiting for transfers between devices: 9.63 us -> 0.01 us  [body(): feed_g = lax.all_gather(feed_g.reshape(piece), 'seq', axis=0)[:inner]]
    ppermute x4, starting transfers between devices: 10.5 us -> 19.6 us  [shift(): return lax.ppermute(x, 'tp', pairs)]
    all_to_all x1, waiting for transfers between devices: 8.91 us -> 15.6 us  [own_shard(): got = lax.all_to_all(total, 'tp', 0, 0, tiled=True)]
    ppermute x22 -> x32, starting transfers between devices: 17 us -> 22.2 us  [swap(): return lax.ppermute(x, 'seq', [(i, i ^ mask) for i in range(n_seq)])]
    all_to_all x2, waiting for transfers between devices: 29.5 us -> 25.4 us  [over_tp(): return lax.all_to_all(block, 'tp', 0, 0, tiled=True)]
  transfers between devices with their start and end apart: 32 -> 41, of which waited for: 15 -> 18; matrix products, arithmetic and copies ran while one was open for 5% -> 9% of each run, Pallas kernels for 17% -> 25%
where the time goes in v1:
time: 297 us; the launch traced here: 293 us
  Pallas kernels  102 us (34%)
  waiting for transfers between devices  85.7 us (29%)
  starting transfers between devices  58.1 us (20%)
  other arithmetic  16.3 us (5%)
  between operations  15.7 us (5%)
  local copies, waits for them, and re-layouts  15 us (5%)
    pallas_call x9, Pallas kernels, call(): pl.pallas_call(kernel, out_shape=tuple((jax.ShapeDtypeStruct(*o) for o in...  102 us
    ppermute x32, waiting for transfers between devices, swap(): return lax.ppermute(x, 'seq', [(i, i ^ mask) for i in range(n_seq)])  36.2 us
    all_to_all x2, waiting for transfers between devices, over_tp(): return lax.all_to_all(block, 'tp', 0, 0, tiled=True)  25.4 us
    ppermute x32, starting transfers between devices, swap(): return lax.ppermute(x, 'seq', [(i, i ^ mask) for i in range(n_seq)])  22.2 us
    ppermute x4, starting transfers between devices, shift(): return lax.ppermute(x, 'tp', pairs)  19.6 us
    all_to_all x1, waiting for transfers between devices, own_shard(): got = lax.all_to_all(total, 'tp', 0, 0, tiled=True)  15.6 us
    convert_element_type x8, other arithmetic, core_sums(): (k.astype(F32) + g.astype(F32)).astype(BF16)  10.9 us
    all_to_all x2, starting transfers between devices, over_tp(): return lax.all_to_all(block, 'tp', 0, 0, tiled=True)  9.81 us
  transfers between devices with their start and end apart: 41, of which 18 were waited for; matrix products, arithmetic and copies ran while one was open for 9% of the time, Pallas kernels for 25%

profile of v1, /device:TPU:0, one launch (start us, length us, event | category | flops | bytes accessed | tf_op | source)
XLA Modules:
  0.0 292.9 jit_solution(12238660115559888411)
XLA Ops:
  7.2 0.7 subtract_convert_fusion
  7.9 0.8 dynamic-slice_bitcast_fusion.7
  8.8 0.9 dynamic-slice_bitcast_fusion.5
  9.9 1.0 broadcast_in_dim.16
  10.9 6.3 %all-to-all-start = ((bf16[4,3,144,256]{3,2,1,0:T(8,128)(2,1)}), bf16[4,3,144,256]{3,2,1,0:T(8,128)(2,1)S(1)}, u32[]{:S(2)}, u32[]{:S(2)}) async-start(bf16[4,3,144,256]{3,2,1,0:T(8,128)(2,1)} %broadcast_in_dim.16), calls=%async_computation | async-start | bytes 1769472 | tf_op jit(solution)/shard_map/all_to_all | solution.py:757
  17.2 0.8 constant_dynamic-slice_fusion.3
  18.5 21.0 %all-to-all-done = bf16[4,3,144,256]{3,2,1,0:T(8,128)(2,1)S(1)} async-done(((bf16[4,3,144,256]{3,2,1,0:T(8,128)(2,1)}), bf16[4,3,144,256]{3,2,1,0:T(8,128)(2,1)S(1)}, u32[]{:S(2)}, u32[]{:S(2)}) %all-to-all-start) | async-done | bytes 884768 | tf_op jit(solution)/shard_map/all_to_all | solution.py:757
  39.4 0.9 broadcast_in_dim.17
  40.4 3.5 %all-to-all-start.1 = ((bf16[4,3,128,256]{3,2,1,0:T(8,128)(2,1)}), bf16[4,3,128,256]{3,2,1,0:T(8,128)(2,1)S(1)}, u32[]{:S(2)}, u32[]{:S(2)}) async-start(bf16[4,3,128,256]{3,2,1,0:T(8,128)(2,1)} %broadcast_in_dim.17), calls=%async_computation.1 | async-start | bytes 1572864 | tf_op jit(solution)/shard_map/all_to_all | solution.py:757
  44.2 1.6 collective-permute-start.6
  46.4 1.6 collective-permute-start.4
  48.5 10.5 %collective-permute-done.6.refs_14_.refs_9_.refs_15_ = bf16[3,3,128,256]{3,2,1,0:T(8,128)(2,1)} collective-permute-done((bf16[3,3,128,256]{3,2,1,0:T(8,128)(2,1)S(1)}, bf16[3,3,128,256]{3,2,1,0:T(8,128)(2,1)}, u32[]{:S(2)}, u32[]{:S(2)}) %collective-permute-start.6) | collective-permute-done | bytes 589856 | tf_op jit(solution)/shard_map/ppermute | solution.py:737
  59.1 4.4 %all-to-all-done.1 = bf16[4,3,128,256]{3,2,1,0:T(8,128)(2,1)S(1)} async-done(((bf16[4,3,128,256]{3,2,1,0:T(8,128)(2,1)}), bf16[4,3,128,256]{3,2,1,0:T(8,128)(2,1)S(1)}, u32[]{:S(2)}, u32[]{:S(2)}) %all-to-all-start.1) | async-done | bytes 786464 | tf_op jit(solution)/shard_map/all_to_all | solution.py:757
  63.5 1.3 collective-permute-start.1
  64.8 5.6 %collective-permute-start = (bf16[512,1024]{1,0:T(8,128)(2,1)}, bf16[512,1024]{1,0:T(8,128)(2,1)}, u32[]{:S(2)}, u32[]{:S(2)}) collective-permute-start(bf16[512,1024]{1,0:T(8,128)(2,1)} %inputs.3), channel_id=1, source_target_pairs={{0,1},{1,2},{2,3},{4,5},{5,6},{6,7},{8,9},{9,10},{10,11},{12,13},{... | collective-permute-start | bytes 3145736 | tf_op jit(solution)/shard_map/ppermute | solution.py:734
  71.2 1.0 copy.54
  72.2 1.0 copy.55
  73.2 1.1 broadcast_in_dim.43.segk
  76.5 2.5 collective-permute-done.5.refs_13_.refs_8_.refs_14_
  79.0 2.4 collective-permute-start.11
  82.5 7.2 %collective-permute-done.1.refs_6_.refs_5_ = bf16[512,1024]{1,0:T(8,128)(2,1)} collective-permute-done((bf16[512,1024]{1,0:T(8,128)(2,1)}, bf16[512,1024]{1,0:T(8,128)(2,1)}, u32[]{:S(2)}, u32[]{:S(2)}) %collective-permute-start.1) | collective-permute-done | bytes 1048608 | tf_op jit(solution)/shard_map/ppermute | solution.py:734
  89.8 1.2 collective-permute-done.refs_4_.refs_3_
  91.0 19.2 %forward_attention.1 = (bf16[512,1024]{1,0:T(8,128)(2,1)}, f32[8,512]{1,0:T(8,128)}, bf16[512,1024]{1,0:T(8,128)(2,1)}, bf16[1536,1024]{1,0:T(8,128)(2,1)}, bf16...) custom-call(s32[2]{0:T(128)} %pad_add_fusion.1.meta, s32[2,2]{1,0:T(2,128)} %pad_add_fusion.rng, s32[1,512]{1,0:T(1,128)} %bitcast.87, ...), custom_call_target="tpu_custom_call" | custom-call | flops 49999998976 | bytes 1000000 | tf_op jit(solution)/shard_map/forward_attention/pallas_call | solution.py:54
  111.4 1.0 collective-permute-done.12.refs_5_
  112.3 0.8 collective-permute-done.13.refs_7_
  113.2 0.8 collective-permute-done.14.refs_9_
  114.0 0.8 collective-permute-done.15.refs_11_
  114.9 0.8 copy-done.30
  115.7 21.8 %feed_forward.1 = (bf16[512,1024]{1,0:T(8,128)(2,1)}, f32[8,512]{1,0:T(8,128)}, f32[8,1024]{1,0:T(8,128)}, bf16[512,1024]{1,0:T(8,128)(2,1)}, f32[512,1024]{1,0:...) custom-call(s32[2]{0:T(128)} %pad_add_fusion.1.meta, ...), custom_call_target="tpu_custom_call" | custom-call | flops 49999998976 | bytes 1000000 | tf_op jit(solution)/shard_map/feed_forward/pallas_call | solution.py:54
  138.6 1.5 collective-permute-done.16
  140.1 1.3 add_convert_fusion.9
  141.7 1.6 collective-permute-start.19
  143.5 2.5 collective-permute-start.21
  146.2 0.8 collective-permute-start.23
  146.9 24.0 %backward_attention.1 = (f32[8,1024]{1,0:T(8,128)}, bf16[512,1024]{1,0:T(8,128)(2,1)}, bf16[1536,1024]{1,0:T(8,128)(2,1)}, bf16[1536,1024]{1,0:T(8,128)(2,1)}, b...) custom-call(s32[2]{0:T(128)} %pad_add_fusion.1.meta, s32[2,2]{1,0:T(2,128)} %pad_add_fusion.rng, ...), custom_call_target="tpu_custom_call" | custom-call | flops 49999998976 | bytes 1000000 | tf_op jit(solution)/shard_map/backward_attention/pallas_call | solution.py:54
  171.0 1.4 slice.226
  172.3 7.6 %collective-permute-done.21 = bf16[4,3,128,256]{3,2,1,0:T(8,128)(2,1)S(1)} collective-permute-done((bf16[4,3,128,256]{3,2,1,0:T(8,128)(2,1)S(1)}, bf16[4,3,128,256]{3,2,1,0:T(8,128)(2,1)S(1)}, u32[]{:S(2)}, u32[]{:S(2)}) %collective-permute-start.21) | collective-permute-done | bytes 786464 | tf_op jit(solution)/shard_map/ppermute | solution.py:737
  179.9 0.8 collective-permute-done.23
  180.8 1.3 add_convert_fusion.5
  182.2 1.5 pause.1
  184.0 2.2 fusion
  186.2 2.2 fusion.1
  188.5 2.2 fusion.2
  190.7 2.2 fusion.3
  192.9 0.8 collective-permute-start.24
  193.8 1.8 collective-permute-start.25
  195.5 0.9 collective-permute-start.26
  196.4 9.7 %halo_grads.1 = (bf16[512,1024]{1,0:T(8,128)(2,1)}, bf16[512,1024]{1,0:T(8,128)(2,1)}) custom-call(s32[2]{0:T(128)} %pad_add_fusion.1.meta, s32[2,2]{1,0:T(2,128)} %pad_add_fusion.rng, bf16[1536,1024]{1,0:T(8,128)(2,1)} %get-tuple-element.145.refs_0_.refs_1_, bf16[1536,1024]{1,0:T(8,128)(2,1)} %get-tuple-element.146.refs_1_.refs_2_, ...), custom_call_target="tpu_custom_call" | custom-call | flops 49999998976 | bytes 1000000 | tf_op jit(solution)/shard_map/halo_grads/pallas_call | solution.py:54
  206.2 1.3 collective-permute-start.28
  207.5 11.4 %collective-permute-start.27 = (bf16[512,1024]{1,0:T(8,128)(2,1)}, bf16[512,1024]{1,0:T(8,128)(2,1)}, u32[]{:S(2)}, u32[]{:S(2)}) collective-permute-start(bf16[512,1024]{1,0:T(8,128)(2,1)} %get-tuple-element.148.refs_7_), channel_id=1, source_target_pairs={{0,1},{1,2},{2,3},{4,5},{5,6},{6,7},{8,9},{9,10},{10,11},{12,13},{... | collective-permute-start | bytes 3145736 | tf_op jit(solution)/shard_map/ppermute | solution.py:734
  218.9 13.0 %input_grads.1 = (f32[512,1024]{1,0:T(8,128)}, f32[8,1024]{1,0:T(8,128)}) custom-call(s32[2]{0:T(128)} %pad_add_fusion.1.meta, s32[2,2]{1,0:T(2,128)} %pad_add_fusion.rng, bf16[512,1024]{1,0:T(8,128)(2,1)} %get-tuple-element.144.refs_0_, bf16[1536,1024]{1,0:T(8,128)(2,1)} %get-tuple-element.145.refs_0_.refs_1_, ...), custom_call_target="tpu_custom_call" | custom-call | flops 49999998976 | bytes 1000000 | tf_op jit(solution)/shard_map/input_grads/pallas_call | solution.py:54
  232.0 0.8 slice.227
  233.4 1.0 pad_maximum_fusion
  234.3 6.3 %all-to-all-start.2 = ((bf16[4,3,144,256]{3,2,1,0:T(8,128)(2,1)}), bf16[4,3,144,256]{3,2,1,0:T(8,128)(2,1)S(1)}, u32[]{:S(2)}, u32[]{:S(2)}) async-start(bf16[4,3,144,256]{3,2,1,0:T(8,128)(2,1)} %pad_maximum_fusion), calls=%async_computation.3 | async-start | bytes 1769472 | tf_op jit(solution)/shard_map/all_to_all | solution.py:793
  240.7 5.9 %input_norm_grads.1 = bf16[512,1024]{1,0:T(8,128)(2,1)} custom-call(bf16[512,1024]{1,0:T(8,128)(2,1)} %inputs.3, f32[512,1024]{1,0:T(8,128)} %get-tuple-element.158.g_resid, bf16[512,1024]{1,0:T(8,128)(2,1)} %collective-permute-done.27.from_left, bf16[512,1024]{1,0:T(8,128)(2,1)} %collective-permute-done.28.from_right, f32[1,1024]{1,0:T(1,128)} %bitcast.98, ...), custom_call_target="tpu_custom_call" | custom-call | flops 49999998976 | bytes 1000000 | tf_op jit(solution)/shard_map/input_norm_grads/pallas_call | solution.py:54
  246.6 15.6 %all-to-all-done.2 = bf16[4,3,144,256]{3,2,1,0:T(8,128)(2,1)S(1)} async-done(((bf16[4,3,144,256]{3,2,1,0:T(8,128)(2,1)}), bf16[4,3,144,256]{3,2,1,0:T(8,128)(2,1)S(1)}, u32[]{:S(2)}, u32[]{:S(2)}) %all-to-all-start.2) | async-done | bytes 884768 | tf_op jit(solution)/shard_map/all_to_all | solution.py:793
  262.3 1.5 collective-permute-start.34
  263.8 0.6 collective-permute-start.32
  264.4 1.5 collective-permute-start.30
  265.9 5.8 %collective-permute-done.34.refs_6_ = bf16[3,144,256]{2,1,0:T(8,128)(2,1)S(1)} collective-permute-done((bf16[3,144,256]{2,1,0:T(8,128)(2,1)S(1)}, bf16[3,144,256]{2,1,0:T(8,128)(2,1)S(1)}, u32[]{:S(2)}, u32[]{:S(2)}) %collective-permute-start.34) | collective-permute-done | bytes 221216 | tf_op jit(solution)/shard_map/ppermute | solution.py:737
  271.7 2.7 collective-permute-done.32.refs_4_
  275.0 0.9 collective-permute-done.33.refs_5_
  278.8 3.5 %lay_out_grads.2 = (f32[256,1024]{1,0:T(8,128)}, f32[1024,256]{1,0:T(8,128)}, f32[256,1024]{1,0:T(8,128)}) custom-call(s32[2]{0:T(128)} %pad_add_fusion.1.meta, bf16[8,3,128,256]{3,2,1,0:T(8,128)(2,1)} %all-gather.2.cloned.1.call-done.refs_0_), custom_call_target="tpu_custom_call" | custom-call | flops 49999998976 | bytes 1000000 | tf_op jit(solution)/shard_map/lay_out_grads/pallas_call | solution.py:54
  282.4 3.4 %lay_out_grads.3 = (f32[1024,256]{1,0:T(8,128)}, f32[1024,256]{1,0:T(8,128)}, f32[1024,256]{1,0:T(8,128)}) custom-call(s32[2]{0:T(128)} %pad_add_fusion.1.meta, bf16[3,144,256]{2,1,0:T(8,128)(2,1)} %copy-done.9, bf16[3,144,256]{2,1,0:T(8,128)(2,1)} %copy-done.16, bf16[3,144,256]{2,1,0:T(8,128)(2,1)} %copy-done.15, bf16[3,144,256]{2,1,0:T(8,128)(2,1)} %copy-done.19, ...), custom_call_target="tpu_custom_call" | custom-call | flops 49999998976 | bytes 1000000 | tf_op jit(solution)/shard_map/lay_out_grads/pallas_call | solution.py:54
  (156 shorter events, 12.9 us)
Async XLA Ops:
  9.9 8.3 %copy-start.5 = (bf16[256,1024]{1,0:T(8,128)(2,1)S(1)}, bf16[256,1024]{1,0:T(8,128)(2,1)}, u32[]{:S(2)}) copy-start(bf16[256,1024]{1,0:T(8,128)(2,1)} %param.29) | copy-start | bytes 1572868
  9.9 8.3 %copy-start.6 = (bf16[256,1024]{1,0:T(8,128)(2,1)S(1)}, bf16[256,1024]{1,0:T(8,128)(2,1)}, u32[]{:S(2)}) copy-start(bf16[256,1024]{1,0:T(8,128)(2,1)} %param.35) | copy-start | bytes 1572868
  10.9 28.5 %all-to-all-start = ((bf16[4,3,144,256]{3,2,1,0:T(8,128)(2,1)}), bf16[4,3,144,256]{3,2,1,0:T(8,128)(2,1)S(1)}, u32[]{:S(2)}, u32[]{:S(2)}) async-start(bf16[4,3,144,256]{3,2,1,0:T(8,128)(2,1)} %broadcast_in_dim.16), calls=%async_computation | async-start | bytes 1769472 | tf_op jit(solution)/shard_map/all_to_all | solution.py:757
  40.4 23.1 %all-to-all-start.1 = ((bf16[4,3,128,256]{3,2,1,0:T(8,128)(2,1)}), bf16[4,3,128,256]{3,2,1,0:T(8,128)(2,1)S(1)}, u32[]{:S(2)}, u32[]{:S(2)}) async-start(bf16[4,3,128,256]{3,2,1,0:T(8,128)(2,1)} %broadcast_in_dim.17), calls=%async_computation.1 | async-start | bytes 1572864 | tf_op jit(solution)/shard_map/all_to_all | solution.py:757
  43.9 188.0 %reduce-scatter.2.cloned.1.call-start = ((), (), s32[]{:S(2)}) async-start(), calls=%async_computation.4 | async-start | bytes 983040 | tf_op jit(solution)/shard_map/reduce_scatter | solution.py:902
  44.2 32.3 %copy-start.7 = (bf16[3,3,128,256]{3,2,1,0:T(8,128)(2,1)}, bf16[3,3,128,256]{3,2,1,0:T(8,128)(2,1)S(1)}, u32[]{:S(2)}) copy-start(bf16[3,3,128,256]{3,2,1,0:T(8,128)(2,1)S(1)} %pad_maximum_fusion.1.refs_10_.refs_5_.refs_11_) | copy-start | bytes 1769476
  44.2 14.8 %collective-permute-start.6 = (bf16[3,3,128,256]{3,2,1,0:T(8,128)(2,1)S(1)}, bf16[3,3,128,256]{3,2,1,0:T(8,128)(2,1)}, u32[]{:S(2)}, u32[]{:S(2)}) collective-permute-start(bf16[3,3,128,256]{3,2,1,0:T(8,128)(2,1)S(1)} %pad_maximum_fusion.1.refs_10_.refs_5_.refs_11_), channel_id=1, source_target_pairs={{0,16},{4,20},{8,24},{12,28},{16,0},{20,4},{24,8},{28,12},{1,17},{... | collective-permute-start | bytes 1769480 | tf_op jit(solution)/shard_map/ppermute | solution.py:737
  46.4 28.7 %collective-permute-start.4 = (bf16[3,3,128,256]{3,2,1,0:T(8,128)(2,1)S(1)}, bf16[3,3,128,256]{3,2,1,0:T(8,128)(2,1)}, u32[]{:S(2)}, u32[]{:S(2)}) collective-permute-start(bf16[3,3,128,256]{3,2,1,0:T(8,128)(2,1)S(1)} %pad_maximum_fusion.1.refs_10_.refs_5_.refs_11_), channel_id=1, source_target_pairs={{0,8},{4,12},{8,0},{12,4},{16,24},{20,28},{24,16},{28,20},{1,9},{5... | collective-permute-start | bytes 1769480 | tf_op jit(solution)/shard_map/ppermute | solution.py:737
  48.0 27.1 %collective-permute-start.2 = (bf16[3,3,128,256]{3,2,1,0:T(8,128)(2,1)S(1)}, bf16[3,3,128,256]{3,2,1,0:T(8,128)(2,1)}, u32[]{:S(2)}, u32[]{:S(2)}) collective-permute-start(bf16[3,3,128,256]{3,2,1,0:T(8,128)(2,1)S(1)} %pad_maximum_fusion.1.refs_10_.refs_5_.refs_11_), channel_id=1, source_target_pairs={{0,24},{4,28},{8,16},{12,20},{16,8},{20,12},{24,0},{28,4},{1,25},{... | collective-permute-start | bytes 1769480 | tf_op jit(solution)/shard_map/ppermute | solution.py:737
  59.0 16.7 %collective-permute-start.7 = (bf16[3,3,128,256]{3,2,1,0:T(8,128)(2,1)}, bf16[3,3,128,256]{3,2,1,0:T(8,128)(2,1)}, u32[]{:S(2)}, u32[]{:S(2)}) collective-permute-start(bf16[3,3,128,256]{3,2,1,0:T(8,128)(2,1)} %collective-permute-done.6.refs_14_.refs_9_.refs_15_), channel_id=1, source_target_pairs={{0,4},{4,0},{8,12},{12,8},{16,20},{20,16},{24,28},{28,24},{1,5},{5... | collective-permute-start | bytes 1769480 | tf_op jit(solution)/shard_map/ppermute | solution.py:737
  63.5 26.3 %collective-permute-start.1 = (bf16[512,1024]{1,0:T(8,128)(2,1)}, bf16[512,1024]{1,0:T(8,128)(2,1)}, u32[]{:S(2)}, u32[]{:S(2)}) collective-permute-start(bf16[512,1024]{1,0:T(8,128)(2,1)} %inputs.3), channel_id=1, source_target_pairs={{1,0},{2,1},{3,2},{5,4},{6,5},{7,6},{9,8},{10,9},{11,10},{13,12},{... | collective-permute-start | bytes 3145736 | tf_op jit(solution)/shard_map/ppermute | solution.py:734
  64.8 26.2 %collective-permute-start = (bf16[512,1024]{1,0:T(8,128)(2,1)}, bf16[512,1024]{1,0:T(8,128)(2,1)}, u32[]{:S(2)}, u32[]{:S(2)}) collective-permute-start(bf16[512,1024]{1,0:T(8,128)(2,1)} %inputs.3), channel_id=1, source_target_pairs={{0,1},{1,2},{2,3},{4,5},{5,6},{6,7},{8,9},{9,10},{10,11},{12,13},{... | collective-permute-start | bytes 3145736 | tf_op jit(solution)/shard_map/ppermute | solution.py:734
  71.0 5.5 %copy-start.20 = (s32[512]{0:T(512)}, s32[512]{0:T(512)S(1)}, u32[]{:S(2)}) copy-start(s32[512]{0:T(512)S(1)} %slice.177) | copy-start | bytes 6148
  75.1 6.4 %collective-permute-start.3 = (bf16[3,3,128,256]{3,2,1,0:T(8,128)(2,1)S(1)}, bf16[3,3,128,256]{3,2,1,0:T(8,128)(2,1)S(1)}, u32[]{:S(2)}, u32[]{:S(2)}) collective-permute-start(bf16[3,3,128,256]{3,2,1,0:T(8,128)(2,1)S(1)} %pad_maximum_fusion.1.refs_10_.refs_5_.refs_11_), channel_id=1, source_target_pairs={{0,4},{4,0},{8,12},{12,8},{16,20},{20,16},{24,28},{28,24},{1,5},{5... | collective-permute-start | bytes 1769480 | tf_op jit(solution)/shard_map/ppermute | solution.py:737
  75.2 6.9 %collective-permute-start.8 = (bf16[3,3,128,256]{3,2,1,0:T(8,128)(2,1)}, bf16[3,3,128,256]{3,2,1,0:T(8,128)(2,1)S(1)}, u32[]{:S(2)}, u32[]{:S(2)}) collective-permute-start(bf16[3,3,128,256]{3,2,1,0:T(8,128)(2,1)} %collective-permute-done.2.refs_16_.refs_11_.refs_17_), channel_id=1, source_target_pairs={{0,4},{4,0},{8,12},{12,8},{16,20},{20,16},{24,28},{28,24},{1,5},{5... | collective-permute-start | bytes 1769480 | tf_op jit(solution)/shard_map/ppermute | solution.py:737
  75.7 3.4 %collective-permute-start.5 = (bf16[3,3,128,256]{3,2,1,0:T(8,128)(2,1)}, bf16[3,3,128,256]{3,2,1,0:T(8,128)(2,1)S(1)}, u32[]{:S(2)}, u32[]{:S(2)}) collective-permute-start(bf16[3,3,128,256]{3,2,1,0:T(8,128)(2,1)} %collective-permute-done.4.refs_12_.refs_7_.refs_13_), channel_id=1, source_target_pairs={{0,4},{4,0},{8,12},{12,8},{16,20},{20,16},{24,28},{28,24},{1,5},{5... | collective-permute-start | bytes 1769480 | tf_op jit(solution)/shard_map/ppermute | solution.py:737
  76.5 33.7 %copy-start.8 = (bf16[3,3,128,256]{3,2,1,0:T(8,128)(2,1)}, bf16[3,3,128,256]{3,2,1,0:T(8,128)(2,1)S(1)}, u32[]{:S(2)}) copy-start(bf16[3,3,128,256]{3,2,1,0:T(8,128)(2,1)S(1)} %pad_maximum_fusion.2.refs_4_) | copy-start | bytes 1769476
  79.0 11.9 %copy-start.23 = (bf16[3,3,128,256]{3,2,1,0:T(8,128)(2,1)}, bf16[3,3,128,256]{3,2,1,0:T(8,128)(2,1)S(1)}, u32[]{:S(2)}) copy-start(bf16[3,3,128,256]{3,2,1,0:T(8,128)(2,1)S(1)} %collective-permute-done.5.refs_13_.refs_8_.refs_14_) | copy-start | bytes 1769476
  79.0 31.1 %collective-permute-start.11 = (bf16[3,3,128,256]{3,2,1,0:T(8,128)(2,1)S(1)}, bf16[3,3,128,256]{3,2,1,0:T(8,128)(2,1)S(1)}, u32[]{:S(2)}, u32[]{:S(2)}) collective-permute-start(bf16[3,3,128,256]{3,2,1,0:T(8,128)(2,1)S(1)} %pad_maximum_fusion.2.refs_4_), channel_id=1, source_target_pairs={{0,24},{4,28},{8,16},{12,20},{16,8},{20,12},{24,0},{28,4},{1,25},{... | collective-permute-start | bytes 1769480 | tf_op jit(solution)/shard_map/ppermute | solution.py:737
  81.5 9.5 %copy-start.21 = (bf16[3,3,128,256]{3,2,1,0:T(8,128)(2,1)}, bf16[3,3,128,256]{3,2,1,0:T(8,128)(2,1)S(1)}, u32[]{:S(2)}) copy-start(bf16[3,3,128,256]{3,2,1,0:T(8,128)(2,1)S(1)} %collective-permute-done.3.refs_11_.refs_6_.refs_12_) | copy-start | bytes 1769476
  81.5 28.7 %collective-permute-start.10 = (bf16[3,3,128,256]{3,2,1,0:T(8,128)(2,1)S(1)}, bf16[3,3,128,256]{3,2,1,0:T(8,128)(2,1)S(1)}, u32[]{:S(2)}, u32[]{:S(2)}) collective-permute-start(bf16[3,3,128,256]{3,2,1,0:T(8,128)(2,1)S(1)} %pad_maximum_fusion.2.refs_4_), channel_id=1, source_target_pairs={{0,16},{4,20},{8,24},{12,28},{16,0},{20,4},{24,8},{28,12},{1,17},{... | collective-permute-start | bytes 1769480 | tf_op jit(solution)/shard_map/ppermute | solution.py:737
  82.0 9.0 %copy-start.22 = (bf16[3,3,128,256]{3,2,1,0:T(8,128)(2,1)}, bf16[3,3,128,256]{3,2,1,0:T(8,128)(2,1)S(1)}, u32[]{:S(2)}) copy-start(bf16[3,3,128,256]{3,2,1,0:T(8,128)(2,1)S(1)} %collective-permute-done.8.refs_17_.refs_12_.refs_18_) | copy-start | bytes 1769476
  82.0 28.2 %collective-permute-start.9 = (bf16[3,3,128,256]{3,2,1,0:T(8,128)(2,1)S(1)}, bf16[3,3,128,256]{3,2,1,0:T(8,128)(2,1)S(1)}, u32[]{:S(2)}, u32[]{:S(2)}) collective-permute-start(bf16[3,3,128,256]{3,2,1,0:T(8,128)(2,1)S(1)} %pad_maximum_fusion.2.refs_4_), channel_id=1, source_target_pairs={{0,8},{4,12},{8,0},{12,4},{16,24},{20,28},{24,16},{28,20},{1,9},{5... | collective-permute-start | bytes 1769480 | tf_op jit(solution)/shard_map/ppermute | solution.py:737
  110.2 4.7 %copy-start.24 = (bf16[3,3,128,256]{3,2,1,0:T(8,128)(2,1)}, bf16[3,3,128,256]{3,2,1,0:T(8,128)(2,1)S(1)}, u32[]{:S(2)}) copy-start(bf16[3,3,128,256]{3,2,1,0:T(8,128)(2,1)S(1)} %collective-permute-done.11.refs_10_) | copy-start | bytes 1769476
  110.2 4.6 %copy-start.25 = (bf16[3,3,128,256]{3,2,1,0:T(8,128)(2,1)}, bf16[3,3,128,256]{3,2,1,0:T(8,128)(2,1)S(1)}, u32[]{:S(2)}) copy-start(bf16[3,3,128,256]{3,2,1,0:T(8,128)(2,1)S(1)} %collective-permute-done.10.refs_8_) | copy-start | bytes 1769476
  110.2 4.6 %copy-start.26 = (bf16[3,3,128,256]{3,2,1,0:T(8,128)(2,1)}, bf16[3,3,128,256]{3,2,1,0:T(8,128)(2,1)S(1)}, u32[]{:S(2)}) copy-start(bf16[3,3,128,256]{3,2,1,0:T(8,128)(2,1)S(1)} %collective-permute-done.9.refs_6_) | copy-start | bytes 1769476
  110.3 2.1 collective-permute-start.12
  110.3 2.8 collective-permute-start.13
  110.8 3.2 %collective-permute-start.14 = (bf16[3,3,128,256]{3,2,1,0:T(8,128)(2,1)S(1)}, bf16[3,3,128,256]{3,2,1,0:T(8,128)(2,1)S(1)}, u32[]{:S(2)}, u32[]{:S(2)}) collective-permute-start(bf16[3,3,128,256]{3,2,1,0:T(8,128)(2,1)S(1)} %collective-permute-done.10.refs_8_), channel_id=1, source_target_pairs={{0,4},{4,0},{8,12},{12,8},{16,20},{20,16},{24,28},{28,24},{1,5},{5... | collective-permute-start | bytes 1769480 | tf_op jit(solution)/shard_map/ppermute | solution.py:737
  110.9 3.9 %collective-permute-start.15 = (bf16[3,3,128,256]{3,2,1,0:T(8,128)(2,1)S(1)}, bf16[3,3,128,256]{3,2,1,0:T(8,128)(2,1)S(1)}, u32[]{:S(2)}, u32[]{:S(2)}) collective-permute-start(bf16[3,3,128,256]{3,2,1,0:T(8,128)(2,1)S(1)} %collective-permute-done.11.refs_10_), channel_id=1, source_target_pairs={{0,4},{4,0},{8,12},{12,8},{16,20},{20,16},{24,28},{28,24},{1,5},{5... | collective-permute-start | bytes 1769480 | tf_op jit(solution)/shard_map/ppermute | solution.py:737
  137.5 2.6 collective-permute-start.16
  137.7 3.7 %collective-permute-start.18 = (bf16[4,3,128,256]{3,2,1,0:T(8,128)(2,1)}, bf16[4,3,128,256]{3,2,1,0:T(8,128)(2,1)S(1)}, u32[]{:S(2)}, u32[]{:S(2)}) collective-permute-start(bf16[4,3,128,256]{3,2,1,0:T(8,128)(2,1)} %get-tuple-element.125), channel_id=1, source_target_pairs={{0,4},{4,0},{8,12},{12,8},{16,20},{20,16},{24,28},{28,24},{1,5},{5... | collective-permute-start | bytes 2359304 | tf_op jit(solution)/shard_map/ppermute | solution.py:737
  138.1 5.2 %collective-permute-start.20 = (bf16[4,3,128,256]{3,2,1,0:T(8,128)(2,1)}, bf16[4,3,128,256]{3,2,1,0:T(8,128)(2,1)S(1)}, u32[]{:S(2)}, u32[]{:S(2)}) collective-permute-start(bf16[4,3,128,256]{3,2,1,0:T(8,128)(2,1)} %get-tuple-element.127), channel_id=1, source_target_pairs={{0,4},{4,0},{8,12},{12,8},{16,20},{20,16},{24,28},{28,24},{1,5},{5... | collective-permute-start | bytes 2359304 | tf_op jit(solution)/shard_map/ppermute | solution.py:737
  138.2 7.8 %collective-permute-start.22 = (bf16[4,3,128,256]{3,2,1,0:T(8,128)(2,1)}, bf16[4,3,128,256]{3,2,1,0:T(8,128)(2,1)S(1)}, u32[]{:S(2)}, u32[]{:S(2)}) collective-permute-start(bf16[4,3,128,256]{3,2,1,0:T(8,128)(2,1)} %get-tuple-element.129), channel_id=1, source_target_pairs={{0,4},{4,0},{8,12},{12,8},{16,20},{20,16},{24,28},{28,24},{1,5},{5... | collective-permute-start | bytes 2359304 | tf_op jit(solution)/shard_map/ppermute | solution.py:737
  141.7 4.3 %copy-start.2 = (bf16[4,3,128,256]{3,2,1,0:T(8,128)(2,1)S(1)}, bf16[4,3,128,256]{3,2,1,0:T(8,128)(2,1)}, u32[]{:S(2)}) copy-start(bf16[4,3,128,256]{3,2,1,0:T(8,128)(2,1)} %get-tuple-element.128) | copy-start | bytes 2359300
  141.7 30.7 %collective-permute-start.19 = (bf16[4,3,128,256]{3,2,1,0:T(8,128)(2,1)S(1)}, bf16[4,3,128,256]{3,2,1,0:T(8,128)(2,1)S(1)}, u32[]{:S(2)}, u32[]{:S(2)}) collective-permute-start(bf16[4,3,128,256]{3,2,1,0:T(8,128)(2,1)S(1)} %add_convert_fusion.8), channel_id=1, source_target_pairs={{0,8},{4,12},{8,0},{12,4},{16,24},{20,28},{24,16},{28,20},{1,9},{5... | collective-permute-start | bytes 2359304 | tf_op jit(solution)/shard_map/ppermute | solution.py:737
  143.5 36.5 %collective-permute-start.21 = (bf16[4,3,128,256]{3,2,1,0:T(8,128)(2,1)S(1)}, bf16[4,3,128,256]{3,2,1,0:T(8,128)(2,1)S(1)}, u32[]{:S(2)}, u32[]{:S(2)}) collective-permute-start(bf16[4,3,128,256]{3,2,1,0:T(8,128)(2,1)S(1)} %add_convert_fusion.7), channel_id=1, source_target_pairs={{0,16},{4,20},{8,24},{12,28},{16,0},{20,4},{24,8},{28,12},{1,17},{... | collective-permute-start | bytes 2359304 | tf_op jit(solution)/shard_map/ppermute | solution.py:737
  146.2 34.6 %collective-permute-start.23 = (bf16[4,3,128,256]{3,2,1,0:T(8,128)(2,1)S(1)}, bf16[4,3,128,256]{3,2,1,0:T(8,128)(2,1)S(1)}, u32[]{:S(2)}, u32[]{:S(2)}) collective-permute-start(bf16[4,3,128,256]{3,2,1,0:T(8,128)(2,1)S(1)} %add_convert_fusion.6), channel_id=1, source_target_pairs={{0,24},{4,28},{8,16},{12,20},{16,8},{20,12},{24,0},{28,4},{1,25},{... | collective-permute-start | bytes 2359304 | tf_op jit(solution)/shard_map/ppermute | solution.py:737
  172.3 11.4 %collective-permute-start.17 = (bf16[4,4,3,128,256]{4,3,2,1,0:T(8,128)(2,1)}, bf16[4,4,3,128,256]{4,3,2,1,0:T(8,128)(2,1)}, u32[]{:S(2)}, u32[]{:S(2)}) collective-permute-start(bf16[4,4,3,128,256]{4,3,2,1,0:T(8,128)(2,1)} %get-tuple-element.122), channel_id=1, source_target_pairs={{0,4},{4,0},{8,12},{12,8},{16,20},{20,16},{24,28},{28,24},{1,5},{5... | collective-permute-start | bytes 9437192 | tf_op jit(solution)/shard_map/ppermute | solution.py:737
  182.1 96.7 %all-gather.2.cloned.1.call-start = ((), (), s32[]{:S(2)}) async-start(), calls=%async_computation.5 | async-start | bytes 1769472 | tf_op jit(solution)/shard_map/all_gather | solution.py:908
  192.9 39.9 %collective-permute-start.24 = (bf16[4,3,128,256]{3,2,1,0:T(8,128)(2,1)}, bf16[4,3,128,256]{3,2,1,0:T(8,128)(2,1)S(1)}, u32[]{:S(2)}, u32[]{:S(2)}) collective-permute-start(bf16[4,3,128,256]{3,2,1,0:T(8,128)(2,1)} %fusion.2), channel_id=1, source_target_pairs={{0,8},{4,12},{8,0},{12,4},{16,24},{20,28},{24,16},{28,20},{1,9},{5... | collective-permute-start | bytes 2359304 | tf_op jit(solution)/shard_map/ppermute | solution.py:737
  193.8 39.1 %collective-permute-start.25 = (bf16[4,3,128,256]{3,2,1,0:T(8,128)(2,1)}, bf16[4,3,128,256]{3,2,1,0:T(8,128)(2,1)S(1)}, u32[]{:S(2)}, u32[]{:S(2)}) collective-permute-start(bf16[4,3,128,256]{3,2,1,0:T(8,128)(2,1)} %fusion.1), channel_id=1, source_target_pairs={{0,16},{4,20},{8,24},{12,28},{16,0},{20,4},{24,8},{28,12},{1,17},{... | collective-permute-start | bytes 2359304 | tf_op jit(solution)/shard_map/ppermute | solution.py:737
  195.5 37.3 %collective-permute-start.26 = (bf16[4,3,128,256]{3,2,1,0:T(8,128)(2,1)}, bf16[4,3,128,256]{3,2,1,0:T(8,128)(2,1)S(1)}, u32[]{:S(2)}, u32[]{:S(2)}) collective-permute-start(bf16[4,3,128,256]{3,2,1,0:T(8,128)(2,1)} %fusion), channel_id=1, source_target_pairs={{0,24},{4,28},{8,16},{12,20},{16,8},{20,12},{24,0},{28,4},{1,25},{... | collective-permute-start | bytes 2359304 | tf_op jit(solution)/shard_map/ppermute | solution.py:737
  206.2 34.5 %collective-permute-start.28 = (bf16[512,1024]{1,0:T(8,128)(2,1)}, bf16[512,1024]{1,0:T(8,128)(2,1)}, u32[]{:S(2)}, u32[]{:S(2)}) collective-permute-start(bf16[512,1024]{1,0:T(8,128)(2,1)} %get-tuple-element.147.refs_6_), channel_id=1, source_target_pairs={{1,0},{2,1},{3,2},{5,4},{6,5},{7,6},{9,8},{10,9},{11,10},{13,12},{... | collective-permute-start | bytes 3145736 | tf_op jit(solution)/shard_map/ppermute | solution.py:734
  207.5 33.2 %collective-permute-start.27 = (bf16[512,1024]{1,0:T(8,128)(2,1)}, bf16[512,1024]{1,0:T(8,128)(2,1)}, u32[]{:S(2)}, u32[]{:S(2)}) collective-permute-start(bf16[512,1024]{1,0:T(8,128)(2,1)} %get-tuple-element.148.refs_7_), channel_id=1, source_target_pairs={{0,1},{1,2},{2,3},{4,5},{5,6},{6,7},{8,9},{9,10},{10,11},{12,13},{... | collective-permute-start | bytes 3145736 | tf_op jit(solution)/shard_map/ppermute | solution.py:734
  218.9 13.0 %copy-start.11 = (f32[8,1024]{1,0:T(8,128)S(1)}, f32[8,1024]{1,0:T(8,128)}, u32[]{:S(2)}) copy-start(f32[8,1024]{1,0:T(8,128)} %pause.1) | copy-start | bytes 98308
  218.9 13.9 %copy-start.10 = (bf16[2,1024]{1,0:T(2,128)(2,1)S(1)}, bf16[2,1024]{1,0:T(2,128)(2,1)}, u32[]{:S(2)}) copy-start(bf16[2,1024]{1,0:T(2,128)(2,1)} %slice.226) | copy-start | bytes 12292
  218.9 14.0 %copy-start.1 = (bf16[4,3,128,256]{3,2,1,0:T(8,128)(2,1)S(1)}, bf16[4,3,128,256]{3,2,1,0:T(8,128)(2,1)}, u32[]{:S(2)}) copy-start(bf16[4,3,128,256]{3,2,1,0:T(8,128)(2,1)} %fusion.3) | copy-start | bytes 2359300
  234.3 27.8 %all-to-all-start.2 = ((bf16[4,3,144,256]{3,2,1,0:T(8,128)(2,1)}), bf16[4,3,144,256]{3,2,1,0:T(8,128)(2,1)S(1)}, u32[]{:S(2)}, u32[]{:S(2)}) async-start(bf16[4,3,144,256]{3,2,1,0:T(8,128)(2,1)} %pad_maximum_fusion), calls=%async_computation.3 | async-start | bytes 1769472 | tf_op jit(solution)/shard_map/all_to_all | solution.py:793
  262.3 20.0 %copy-start.9 = (bf16[3,144,256]{2,1,0:T(8,128)(2,1)}, bf16[3,144,256]{2,1,0:T(8,128)(2,1)S(1)}, u32[]{:S(2)}) copy-start(bf16[3,144,256]{2,1,0:T(8,128)(2,1)S(1)} %reduce_sum.45.refs_0_) | copy-start | bytes 663556
  262.3 9.4 %collective-permute-start.34 = (bf16[3,144,256]{2,1,0:T(8,128)(2,1)S(1)}, bf16[3,144,256]{2,1,0:T(8,128)(2,1)S(1)}, u32[]{:S(2)}, u32[]{:S(2)}) collective-permute-start(bf16[3,144,256]{2,1,0:T(8,128)(2,1)S(1)} %reduce_sum.45.refs_0_), channel_id=1, source_target_pairs={{0,24},{4,28},{8,16},{12,20},{16,8},{20,12},{24,0},{28,4},{1,25},{... | collective-permute-start | bytes 663560 | tf_op jit(solution)/shard_map/ppermute | solution.py:737
  263.8 10.6 %collective-permute-start.32 = (bf16[3,144,256]{2,1,0:T(8,128)(2,1)S(1)}, bf16[3,144,256]{2,1,0:T(8,128)(2,1)S(1)}, u32[]{:S(2)}, u32[]{:S(2)}) collective-permute-start(bf16[3,144,256]{2,1,0:T(8,128)(2,1)S(1)} %reduce_sum.45.refs_0_), channel_id=1, source_target_pairs={{0,16},{4,20},{8,24},{12,28},{16,0},{20,4},{24,8},{28,12},{1,17},{... | collective-permute-start | bytes 663560 | tf_op jit(solution)/shard_map/ppermute | solution.py:737
  264.4 10.0 %collective-permute-start.30 = (bf16[3,144,256]{2,1,0:T(8,128)(2,1)S(1)}, bf16[3,144,256]{2,1,0:T(8,128)(2,1)S(1)}, u32[]{:S(2)}, u32[]{:S(2)}) collective-permute-start(bf16[3,144,256]{2,1,0:T(8,128)(2,1)S(1)} %reduce_sum.45.refs_0_), channel_id=1, source_target_pairs={{0,8},{4,12},{8,0},{12,4},{16,24},{20,28},{24,16},{28,20},{1,9},{5... | collective-permute-start | bytes 663560 | tf_op jit(solution)/shard_map/ppermute | solution.py:737
  265.9 9.1 %collective-permute-start.29 = (bf16[3,144,256]{2,1,0:T(8,128)(2,1)S(1)}, bf16[3,144,256]{2,1,0:T(8,128)(2,1)S(1)}, u32[]{:S(2)}, u32[]{:S(2)}) collective-permute-start(bf16[3,144,256]{2,1,0:T(8,128)(2,1)S(1)} %reduce_sum.45.refs_0_), channel_id=1, source_target_pairs={{0,4},{4,0},{8,12},{12,8},{16,20},{20,16},{24,28},{28,24},{1,5},{5... | collective-permute-start | bytes 663560 | tf_op jit(solution)/shard_map/ppermute | solution.py:737
  271.7 10.6 %copy-start.13 = (bf16[3,144,256]{2,1,0:T(8,128)(2,1)}, bf16[3,144,256]{2,1,0:T(8,128)(2,1)S(1)}, u32[]{:S(2)}) copy-start(bf16[3,144,256]{2,1,0:T(8,128)(2,1)S(1)} %collective-permute-done.34.refs_6_) | copy-start | bytes 663556
  271.7 3.3 %collective-permute-start.35 = (bf16[3,144,256]{2,1,0:T(8,128)(2,1)S(1)}, bf16[3,144,256]{2,1,0:T(8,128)(2,1)S(1)}, u32[]{:S(2)}, u32[]{:S(2)}) collective-permute-start(bf16[3,144,256]{2,1,0:T(8,128)(2,1)S(1)} %collective-permute-done.34.refs_6_), channel_id=1, source_target_pairs={{0,4},{4,0},{8,12},{12,8},{16,20},{20,16},{24,28},{28,24},{1,5},{5... | collective-permute-start | bytes 663560 | tf_op jit(solution)/shard_map/ppermute | solution.py:737
  274.4 7.9 %copy-start.14 = (bf16[3,144,256]{2,1,0:T(8,128)(2,1)}, bf16[3,144,256]{2,1,0:T(8,128)(2,1)S(1)}, u32[]{:S(2)}) copy-start(bf16[3,144,256]{2,1,0:T(8,128)(2,1)S(1)} %collective-permute-done.32.refs_4_) | copy-start | bytes 663556
  274.4 1.5 collective-permute-start.33
  274.5 7.9 %copy-start.15 = (bf16[3,144,256]{2,1,0:T(8,128)(2,1)}, bf16[3,144,256]{2,1,0:T(8,128)(2,1)S(1)}, u32[]{:S(2)}) copy-start(bf16[3,144,256]{2,1,0:T(8,128)(2,1)S(1)} %collective-permute-done.30.refs_2_) | copy-start | bytes 663556
  274.5 1.8 collective-permute-start.31
  275.0 7.4 %copy-start.16 = (bf16[3,144,256]{2,1,0:T(8,128)(2,1)}, bf16[3,144,256]{2,1,0:T(8,128)(2,1)S(1)}, u32[]{:S(2)}) copy-start(bf16[3,144,256]{2,1,0:T(8,128)(2,1)S(1)} %collective-permute-done.29.refs_1_) | copy-start | bytes 663556
  275.0 7.4 %copy-start.17 = (bf16[3,144,256]{2,1,0:T(8,128)(2,1)}, bf16[3,144,256]{2,1,0:T(8,128)(2,1)S(1)}, u32[]{:S(2)}) copy-start(bf16[3,144,256]{2,1,0:T(8,128)(2,1)S(1)} %collective-permute-done.35.refs_7_) | copy-start | bytes 663556
  275.9 6.5 %copy-start.18 = (bf16[3,144,256]{2,1,0:T(8,128)(2,1)}, bf16[3,144,256]{2,1,0:T(8,128)(2,1)S(1)}, u32[]{:S(2)}) copy-start(bf16[3,144,256]{2,1,0:T(8,128)(2,1)S(1)} %collective-permute-done.33.refs_5_) | copy-start | bytes 663556
  276.2 6.2 %copy-start.19 = (bf16[3,144,256]{2,1,0:T(8,128)(2,1)}, bf16[3,144,256]{2,1,0:T(8,128)(2,1)S(1)}, u32[]{:S(2)}) copy-start(bf16[3,144,256]{2,1,0:T(8,128)(2,1)S(1)} %collective-permute-done.31.refs_3_) | copy-start | bytes 663556
  (8 other events, 16.2 us)
Sparse Core Ops, SparseCore 0:
  182.2 26.2 reduce-scatter.1
  232.1 26.2 all-gather.1
